TPU v7x, 768 devices: a whole 4x8x12 slice. The times are simulated.
768 devices in a mesh: inter: 96 (over y, z_lo, x), intra: 8 (over z_hi, core).
Axes of the slice: x: 4, y: 8, z: 12 (z_hi: 4, z_lo: 3; z = z_hi * 3 + z_lo), core: 2. Of those that a mesh axis runs over, the one named last changes fastest.
Arguments:
- activations: bfloat16 [8, 192, 1, 5120], P('intra'), may hold values from -6 to 6
- hidden_cot: bfloat16 [8, 192, 1, 6912], P('intra', None, None, 'inter'), may hold values from -6 to 6
- weight: float32 [276480, 256], P(('inter', 'intra')), may hold values from -0.078125 to 0.078125
Outputs:
- weight_grad: float32 [276480, 256], P(('inter', 'intra'))
- input_grad: bfloat16 [8, 192, 1, 5120], P('intra', 'inter')
All inputs are finite; a program needn't handle non-finite values. Where the computation divides by a largest or mean magnitude, that divisor is 1e-20 or more.
Results may differ from a plain program's by a relative error of at most 0.024.
Values may be sent and summed in bfloat16 or wider, within the bound.
No kernel may reach another device: no remote copies, remote signals or barrier semaphores. Data moves between devices by JAX's collectives and lax.ppermute only.
A program may use at most 32 MiB of HBM per device.

v0:
```python
import math

import jax
import jax.numpy as jnp
from jax import lax
from jax.sharding import PartitionSpec as P

EPS = 1e-06


def quantize(blocks):
    scales = (jnp.max(jnp.abs(blocks), axis=-1) + EPS).astype(jnp.bfloat16)
    values = (blocks / scales.astype(jnp.float32)[..., None]).astype(jnp.bfloat16)
    return (lax.optimization_barrier(values), scales)


def dequantize(values, scales):
    return values.astype(jnp.float32) * scales.astype(jnp.float32)[..., None]


def body(activations, hidden_cot, weight):
    n_intra = lax.axis_size("intra")
    block_len = weight.shape[1]
    tok_count = activations.shape[1]
    micro = activations.shape[2]
    width = activations.shape[3]
    hidden = hidden_cot.shape[3]
    slab_rows = tok_count * micro
    tokens = activations.reshape(slab_rows, width)
    w_values, w_scales = quantize(weight)
    held_values, held_scales = (
        lax.all_gather(w_values, "intra", axis=0, tiled=True),
        lax.all_gather(w_scales, "intra", axis=0, tiled=True),
    )
    w_matrix = dequantize(held_values, held_scales).astype(jnp.bfloat16).reshape(2 * hidden, width)
    projected = jnp.dot(tokens, w_matrix.T, preferred_element_type=jnp.float32)
    gate = projected[:, :hidden]
    upper = projected[:, hidden:]
    cotangent = hidden_cot.reshape(slab_rows, hidden).astype(jnp.float32)
    sigmoid_gate = jax.nn.sigmoid(gate)
    grad_gate = cotangent * upper * sigmoid_gate * (1.0 + gate * (1.0 - sigmoid_gate))
    grad_up = cotangent * gate * sigmoid_gate
    grad_pre = jnp.concatenate([grad_gate, grad_up], axis=1).astype(jnp.bfloat16)
    partial_rows = jnp.dot(grad_pre, w_matrix, preferred_element_type=jnp.float32)
    summed_rows = lax.psum_scatter(partial_rows, "inter", scatter_dimension=0, tiled=True)
    input_grad = summed_rows.astype(jnp.bfloat16).reshape(1, -1, micro, width)
    local_grad = jnp.einsum(
        "rh,rd->hd", grad_pre, tokens, preferred_element_type=jnp.float32
    ).reshape(-1, block_len)
    g_values, g_scales = quantize(local_grad)
    own_blocks = local_grad.shape[0] // n_intra
    got_values, got_scales = (
        lax.all_to_all(
            g_values.reshape(n_intra, own_blocks, block_len),
            "intra",
            split_axis=0,
            concat_axis=0,
            tiled=True,
        ),
        lax.all_to_all(
            g_scales.reshape(n_intra, own_blocks), "intra", split_axis=0, concat_axis=0, tiled=True
        ),
    )
    summed = jnp.sum(dequantize(got_values, got_scales), axis=0)
    weight_grad = summed * (1.0 / math.sqrt(micro * tok_count * n_intra))
    return (weight_grad, input_grad)


def solution(mesh):
    return jax.shard_map(
        body,
        mesh=mesh,
        in_specs=(
            P("intra", None, None, None),
            P("intra", None, None, "inter"),
            P(("inter", "intra"), None),
        ),
        out_specs=(P(("inter", "intra"), None), P("intra", "inter", None, None)),
        check_vma=False,
    )
```

profile of v0, /device:TPU:192, one launch (start us, length us, event | category | flops | bytes accessed | tf_op | source)
XLA Modules:
  0.0 750.5 jit_solution(9987844858180601579)
XLA Ops:
  7.2 0.0 copy-start
  7.2 0.0 all-gather.2.cloned.1.call-start
  7.2 1.3 abs_reduce_fusion.1
  8.5 1.8 divide_convert_fusion.1
  10.3 0.0 all-gather.2.cloned.1.call-update
  10.3 1.3 dynamic-slice
  12.3 0.3 dynamic-update-slice
  12.5 21.2 %all-reduce = bf16[2880]{0:T(1024)(128)(2,1)S(1)} all-reduce(bf16[2880]{0:T(1024)(128)(2,1)S(1)} %dynamic-update-slice), channel_id=1, replica_groups=mesh['inter'=96,'intra'=8] {'intra'}, use_global_device_ids=true, to_apply=%add | all-reduce | flops 2880 | bytes 11520
  33.7 1.3 dynamic-slice.1
  35.6 25.3 %all-gather.2.cloned.1.call-done = bf16[2880,256]{1,0:T(8,128)(2,1)} async-done(((bf16[360,256]{1,0:T(8,128)(2,1)}), bf16[2880,256]{1,0:T(8,128)(2,1)}) %all-gather.2.cloned.1.call-update) | async-done | bytes 1474576 | tf_op jit(solution)/shard_map/all_gather | solution.py:32
  60.9 2.9 multiply_convert_fusion
  63.8 3.1 reshape.60
  66.9 0.0 copy-start.2
  66.9 0.8 fusion.4
  67.8 2.1 fusion
  70.0 4.3 reshape.62
  74.2 2.5 abs_reduce_fusion
  76.7 0.2 copy-done.1
  77.0 1.6 divide_convert_fusion
  78.6 0.1 convert_element_type.95
  78.7 0.5 broadcast.26
  79.2 0.7 reduce
  79.9 0.7 reshape.73
  80.5 6.0 all-to-all-start.1
  86.5 2.6 fusion.12
  89.1 4.3 all-to-all-done.1
  93.4 6.7 all-to-all-start
  100.1 640.7 %all-reduce.3 = bf16[192,5120]{1,0:T(8,128)(2,1)} all-reduce(f32[192,5120]{1,0:T(8,128)} %fusion.12), channel_id=2, replica_groups=mesh['inter'=96,'intra'=8] {'inter'}, use_global_device_ids=true, to_apply=%region_3.0.clone | all-reduce | flops 983040 | bytes 5898240
  740.8 1.5 fusion.13
  742.3 0.1 reshape.74
  742.4 0.4 multiply_reduce_fusion
  742.9 0.8 broadcast_multiply_fusion
  (10 shorter events, 0.1 us)
Async XLA Ops:
  7.2 59.8 %copy-start = (bf16[1,192,1,5120]{3,1,2,0:T(8,128)(2,1)S(1)}, bf16[1,192,1,5120]{3,1,2,0:T(8,128)(2,1)}, u32[]{:S(2)}) copy-start(bf16[1,192,1,5120]{3,1,2,0:T(8,128)(2,1)} %param.3) | copy-start | bytes 5898244
  7.2 53.7 %all-gather.2.cloned.1.call-start = ((), (), s32[]{:S(2)}) async-start(), calls=%async_computation.2 | async-start | bytes 1658880 | tf_op jit(solution)/shard_map/all_gather | solution.py:32
  66.9 0.8 copy-start.2
  74.2 2.7 copy-start.1
  80.5 12.8 %all-to-all-start.1 = ((bf16[8,2,180]{2,1,0:T(2,128)(2,1)}), bf16[8,2,180]{2,1,0:T(2,128)(2,1)S(1)}, u32[]{:S(2)}, u32[]{:S(2)}) async-start(bf16[8,2,180]{2,1,0:T(2,128)(2,1)} %reshape.73), calls=%async_computation.1 | async-start | bytes 16384 | tf_op jit(solution)/shard_map/all_to_all | solution.py:60
  93.4 649.0 %all-to-all-start = ((bf16[8,360,256]{2,1,0:T(8,128)(2,1)}), bf16[8,360,256]{2,1,0:T(8,128)(2,1)S(1)}, u32[]{:S(2)}, u32[]{:S(2)}) async-start(bf16[8,360,256]{2,1,0:T(8,128)(2,1)} %bitcast.23), calls=%async_computation | async-start | bytes 2949120 | tf_op jit(solution)/shard_map/all_to_all | solution.py:53
Sparse Core Ops, SparseCore 0:
  11.0 49.8 all-gather.1
where the time goes:
time: 751 us; the launch traced here: 750 us
  blocking collectives  662 us (88%)
  waiting for transfers between devices  29.6 us (4%)
  between operations  15.5 us (2%)
  local copies, waits for them, and re-layouts  13.3 us (2%)
  starting transfers between devices  12.8 us (2%)
  other arithmetic  12 us (2%)
    unnamed x2, blocking collectives  662 us
    all_gather x1, waiting for transfers between devices, body(): lax.all_gather(w_values, 'intra', axis=0, tiled=True)  25.3 us
  transfers between devices with their start and end apart: 3, of which 2 were waited for; matrix products, arithmetic and copies ran while one was open for 1% of the time, Pallas kernels for 0%

commit v1 on v0

v1 whole, which is shorter than its diff:
```python
import functools
import math

import jax
import jax.numpy as jnp
from jax import lax
from jax.experimental import pallas as pl
from jax.experimental.pallas import tpu as pltpu
from jax.sharding import Mesh, PartitionSpec as P

EPS = 1e-06
LANES = 128
F32 = jnp.float32
BF16 = jnp.bfloat16
VMEM = pl.BlockSpec(memory_space=pltpu.VMEM)
PARAMS = pltpu.CompilerParams(vmem_limit_bytes=40 << 20)


def requantized(blocks):
    scales = (jnp.max(jnp.abs(blocks), axis=-1, keepdims=True) + EPS).astype(BF16).astype(F32)
    values = (blocks / scales).astype(BF16).astype(F32)
    return values * scales


def quantize_kernel(w_ref, out_ref):
    out_ref[...] = requantized(w_ref[...]).astype(BF16)


def quantize_weight(weight):
    return pl.pallas_call(
        quantize_kernel,
        out_shape=jax.ShapeDtypeStruct(weight.shape, BF16),
        in_specs=[VMEM],
        out_specs=VMEM,
    )(weight)


def permutation(tokens, nx, ny, nz):
    own = tokens // (nx * ny * nz)
    new = lax.broadcasted_iota(jnp.int32, (tokens, tokens), 0)
    old = lax.broadcasted_iota(jnp.int32, (tokens, tokens), 1)
    r = new % own
    y = (new // own) % ny
    z = (new // (own * ny)) % nz
    x = new // (own * ny * nz)
    source = ((y * nz + z) * nx + x) * own + r
    return (source == old).astype(BF16)


def gate_kernel(plan, sizes, pos_ref, *refs):
    pieces, refs = refs[: len(plan)], refs[len(plan) :]
    x_ref, c_ref, perm_ref, part_ref, keep_ref, send_ref, w32, wmat = refs
    zh, core = pos_ref[0], pos_ref[1]
    n_z, chunk = sizes
    rows = wmat.shape[0]
    block = pieces[0].shape[1]
    per_row = w32.shape[1] // rows
    lanes = w32.shape[2]
    halves = block // lanes
    for (dz, dc, first), piece in zip(plan, pieces):
        at = (dc * n_z + lax.rem(zh + dz, n_z)) * chunk + first
        at = pl.multiple_of(at, 8)
        for k in range(halves):
            w32[k, pl.ds(at, piece.shape[0]), :] = piece[:, k * lanes : (k + 1) * lanes].astype(F32)
    proj = jnp.zeros((rows, x_ref.shape[0]), F32)
    for b in range(per_row):
        columns = slice(b * block, (b + 1) * block)
        w = jnp.concatenate(
            [w32[k, pl.ds(b, rows, stride=per_row), :] for k in range(halves)], axis=1
        ).astype(BF16)
        wmat[:, columns] = w
        proj += lax.dot_general(
            w, x_ref[:, columns], (((1,), (1,)), ((), ())), preferred_element_type=F32
        )
    quarter = rows // 4
    eighth = quarter // 2
    cot = c_ref[...].astype(F32).T
    low = jnp.concatenate([cot[:eighth], cot[quarter : quarter + eighth]], axis=0)
    high = jnp.concatenate([cot[eighth:quarter], cot[quarter + eighth :]], axis=0)
    pre = []
    for dc in range(2):
        base = dc * 2 * quarter
        gate = proj[base : base + quarter]
        upper = proj[base + quarter : base + 2 * quarter]
        c = jnp.where(core == dc, low, high)
        sig = jax.nn.sigmoid(gate)
        pre.append(c * upper * sig * (1.0 + gate * (1.0 - sig)))
        pre.append(c * gate * sig)
    keep = jnp.concatenate(pre[:2], axis=0)
    send = jnp.concatenate(pre[2:], axis=0)
    keep_ref[...] = keep.astype(BF16)
    send_ref[...] = send.astype(BF16)
    pre = jnp.concatenate([keep, send], axis=0).astype(BF16)
    pre = lax.dot_general(
        perm_ref[...], pre, (((1,), (1,)), ((), ())), preferred_element_type=F32
    ).astype(BF16)
    for b in range(per_row):
        columns = slice(b * block, (b + 1) * block)
        part_ref[:, columns] = jnp.dot(
            pre, wmat[:, columns], preferred_element_type=F32
        ).astype(BF16)


def gate_part(pos, plan, pieces, n_z, chunk, x, cot, perm):
    tokens, width = x.shape
    rows = 2 * cot.shape[1]
    block = pieces[0].shape[1]
    return pl.pallas_call(
        functools.partial(gate_kernel, plan, (n_z, chunk)),
        out_shape=(
            jax.ShapeDtypeStruct((tokens, width), BF16),
            jax.ShapeDtypeStruct((rows // 2, tokens), BF16),
            jax.ShapeDtypeStruct((rows // 2, tokens), BF16),
        ),
        in_specs=[pl.BlockSpec(memory_space=pltpu.SMEM)] + [VMEM] * (len(pieces) + 3),
        out_specs=(VMEM,) * 3,
        scratch_shapes=[
            pltpu.VMEM((block // LANES, 2 * n_z * chunk, LANES), F32),
            pltpu.VMEM((rows, width), BF16),
        ],
        compiler_params=PARAMS,
    )(pos, *pieces, x, cot, perm)


def weight_grad_kernel(n_z, pos_ref, mine_ref, got_ref, x_ref, xo_ref, own, nxt, prv, far_a, far_b, g32):
    zh = pos_ref[0]
    rows = mine_ref.shape[0]
    chunk, block = own.shape
    per_row = n_z * chunk // rows
    lanes = g32.shape[2]
    for b in range(per_row):
        columns = slice(b * block, (b + 1) * block)
        local = requantized(
            jnp.dot(mine_ref[...], x_ref[:, columns], preferred_element_type=F32)
        ) + requantized(jnp.dot(got_ref[...], xo_ref[:, columns], preferred_element_type=F32))
        for k in range(block // lanes):
            g32[k, pl.ds(b, rows, stride=per_row), :] = local[:, k * lanes : (k + 1) * lanes]
    half = far_a.shape[0]
    for out, dz, first in ((own, 0, 0), (nxt, 1, 0), (prv, n_z - 1, 0), (far_a, 2, 0), (far_b, 2, half)):
        at = pl.multiple_of(lax.rem(zh + dz, n_z) * chunk + first, 8)
        for k in range(block // lanes):
            out[:, k * lanes : (k + 1) * lanes] = g32[k, pl.ds(at, out.shape[0]), :].astype(out.dtype)


def weight_grad_part(pos, mine, got, x, x_other, n_z, chunk, half, block):
    shape = jax.ShapeDtypeStruct
    return pl.pallas_call(
        functools.partial(weight_grad_kernel, n_z),
        out_shape=(
            shape((chunk, block), F32),
            shape((chunk, block), F32),
            shape((chunk, block), F32),
            shape((half, block), BF16),
            shape((chunk - half, block), BF16),
        ),
        in_specs=[pl.BlockSpec(memory_space=pltpu.SMEM)] + [VMEM] * 4,
        out_specs=(VMEM,) * 5,
        scratch_shapes=[pltpu.VMEM((block // LANES, n_z * chunk, LANES), F32)],
        compiler_params=PARAMS,
    )(pos, mine, got, x, x_other)


def relay_kernel(nxt, prv, far_a, far_b, out_nxt, out_prv):
    half = far_a.shape[0]
    out_nxt[:half] = (nxt[:half] + far_a[...].astype(F32)).astype(BF16)
    out_nxt[half:] = nxt[half:].astype(BF16)
    out_prv[:half] = prv[:half].astype(BF16)
    out_prv[half:] = (prv[half:] + far_b[...].astype(F32)).astype(BF16)


def relay(nxt, prv, far_a, far_b):
    return pl.pallas_call(
        relay_kernel,
        out_shape=(jax.ShapeDtypeStruct(nxt.shape, BF16),) * 2,
        in_specs=[VMEM] * 4,
        out_specs=(VMEM,) * 2,
    )(nxt, prv, far_a, far_b)


def step(array, axis, by):
    n = lax.axis_size(axis)
    return lax.ppermute(array, axis, [(i, (i + by) % n) for i in range(n)])


def summed_pieces(array, axis):
    got = lax.all_to_all(array, axis, split_axis=0, concat_axis=0, tiled=True)
    return jnp.sum(got.astype(F32), axis=0).astype(BF16)


def body(activations, hidden_cot, weight):
    tok = activations.shape[1] * activations.shape[2]
    width = activations.shape[3]
    hidden = hidden_cot.shape[3]
    chunk, block = weight.shape
    half = (chunk // 2 + 15) // 16 * 16
    n_x, n_y, n_l, n_z = (lax.axis_size(a) for a in ("x", "y", "zl", "zh"))
    x = activations.reshape(tok, width)
    cot = hidden_cot.reshape(tok, hidden)
    pos = jnp.stack([lax.axis_index("zh"), lax.axis_index("c")]).astype(jnp.int32)
    perm = permutation(tok, n_x, n_y, n_l)

    own = quantize_weight(weight)
    before = step(own, "zh", 1)
    after = step(own, "zh", -1)
    x_other = step(x, "c", 1)
    own_o = step(own, "c", 1)
    far_a = step(before[:half], "zh", 1)
    far_b = step(after[half:], "zh", -1)
    before_o = step(before, "c", 1)
    after_o = step(after, "c", 1)
    far_ao = step(far_a, "c", 1)
    far_bo = step(far_b, "c", 1)
    last = n_z - 1
    plan = ((0, 0, 0), (last, 0, 0), (1, 0, 0), (2, 0, 0), (2, 0, half))
    plan = plan + tuple((dz, 1, first) for dz, _, first in plan)
    pieces = (own, before, after, far_a, far_b, own_o, before_o, after_o, far_ao, far_bo)
    part, keep, send = gate_part(pos, plan, pieces, n_z, chunk, x, cot, perm)

    rows = summed_pieces(part.reshape(n_x, tok // n_x, width), "x")
    rows = summed_pieces(rows.reshape(n_l, -1, width), "zl")
    rows = summed_pieces(rows.reshape(n_y, -1, width), "y")
    input_grad = rows.reshape(1, -1, activations.shape[2], width)

    got = step(send, "c", 1)
    g_own, g_nxt, g_prv, g_fa, g_fb = weight_grad_part(
        pos, keep, got, x, x_other, n_z, chunk, half, block
    )
    r_a = step(g_fa, "zh", 1)
    r_b = step(g_fb, "zh", -1)
    s_nxt, s_prv = relay(g_nxt, g_prv, r_a, r_b)
    from_prv = step(s_nxt, "zh", 1)
    from_nxt = step(s_prv, "zh", -1)
    total = g_own + from_prv.astype(F32) + from_nxt.astype(F32)
    weight_grad = total * (1.0 / math.sqrt(tok * n_z * lax.axis_size("c")))
    return (weight_grad, input_grad)


def solution(mesh):
    fine = Mesh(mesh.devices.reshape(8, 3, 4, 4, 2), ("y", "zl", "x", "zh", "c"))
    inter, intra = ("y", "zl", "x"), ("zh", "c")
    return jax.shard_map(
        body,
        mesh=fine,
        in_specs=(
            P(intra, None, None, None),
            P(intra, None, None, inter),
            P(inter + intra, None),
        ),
        out_specs=(P(inter + intra, None), P(intra, inter, None, None)),
        check_vma=False,
    )
```

time: 751 us -> 150 us (0.20)
  the two profiles are of different devices: /device:TPU:192 before, /device:TPU:128 now
where the time goes in v1:
time: 150 us; the launch traced here: 149 us
  starting transfers between devices  72.6 us (48%)
  waiting for transfers between devices  53.1 us (35%)
  Pallas kernels  9.62 us (6%)
  local copies, waits for them, and re-layouts  7.49 us (5%)
  other arithmetic  5.12 us (3%)
    ppermute x15, starting transfers between devices, step(): return lax.ppermute(array, axis, [(i, (i + by) % n) for i in range(n)])  55.7 us
    all_to_all x3, waiting for transfers between devices, summed_pieces(): got = lax.all_to_all(array, axis, split_axis=0, concat_axis=0, tiled=True)  29.2 us
    ppermute x15, waiting for transfers between devices, step(): return lax.ppermute(array, axis, [(i, (i + by) % n) for i in range(n)])  23.9 us
    all_to_all x3, starting transfers between devices, summed_pieces(): got = lax.all_to_all(array, axis, split_axis=0, concat_axis=0, tiled=True)  16.9 us
    unnamed x17, local copies, waits for them, and re-layouts  6.75 us
    reduce_sum x3, other arithmetic, summed_pieces(): return jnp.sum(got.astype(F32), axis=0).astype(BF16)  3.64 us
    pallas_call x1, Pallas kernels, gate_part(): pl.pallas_call(functools.partial(gate_kernel, plan, (n_z, chunk)), out_sh...  3.1 us
  transfers between devices with their start and end apart: 18, of which 9 were waited for; matrix products, arithmetic and copies ran while one was open for 4% of the time, Pallas kernels for 3%

profile of v1, /device:TPU:128, one launch (start us, length us, event | category | flops | bytes accessed | tf_op | source)
XLA Modules:
  0.0 148.8 jit_solution(4249538347392636474)
XLA Ops:
  0.6 1.8 %shard_map.50.refs_0_ = bf16[360,256]{1,0:T(8,128)(2,1)} custom-call(f32[360,256]{1,0:T(8,128)} %w_ref.1), custom_call_target="tpu_custom_call" | custom-call | tf_op jit(solution)/shard_map/pallas_call | solution.py:30
  2.4 1.9 %collective-permute-start.4 = (bf16[360,256]{1,0:T(8,128)(2,1)}, bf16[360,256]{1,0:T(8,128)(2,1)S(1)}, u32[]{:S(2)}, u32[]{:S(2)}) collective-permute-start(bf16[360,256]{1,0:T(8,128)(2,1)} %shard_map.50.refs_0_), channel_id=1, source_target_pairs={{0,1},{1,0},{2,3},{3,2},{4,5},{5,4},{6,7},{7,6},{8,9},{9,8},{10,11... | collective-permute-start | bytes 552968 | tf_op jit(solution)/shard_map/ppermute | solution.py:182
  4.4 12.8 %collective-permute-start.1 = (bf16[360,256]{1,0:T(8,128)(2,1)}, bf16[360,256]{1,0:T(8,128)(2,1)S(1)}, u32[]{:S(2)}, u32[]{:S(2)}) collective-permute-start(bf16[360,256]{1,0:T(8,128)(2,1)} %shard_map.50.refs_0_), channel_id=1, source_target_pairs={{0,6},{2,0},{4,2},{6,4},{1,7},{3,1},{5,3},{7,5},{8,14},{10,8},{12,... | collective-permute-start | bytes 552968 | tf_op jit(solution)/shard_map/ppermute | solution.py:182
  17.1 1.9 %collective-permute-start = (bf16[360,256]{1,0:T(8,128)(2,1)}, bf16[360,256]{1,0:T(8,128)(2,1)S(1)}, u32[]{:S(2)}, u32[]{:S(2)}) collective-permute-start(bf16[360,256]{1,0:T(8,128)(2,1)} %shard_map.50.refs_0_), channel_id=1, source_target_pairs={{0,2},{2,4},{4,6},{6,0},{1,3},{3,5},{5,7},{7,1},{8,10},{10,12},{12... | collective-permute-start | bytes 552968 | tf_op jit(solution)/shard_map/ppermute | solution.py:182
  19.1 6.9 %collective-permute-done.1.refs_2_ = bf16[360,256]{1,0:T(8,128)(2,1)S(1)} collective-permute-done((bf16[360,256]{1,0:T(8,128)(2,1)}, bf16[360,256]{1,0:T(8,128)(2,1)S(1)}, u32[]{:S(2)}, u32[]{:S(2)}) %collective-permute-start.1) | collective-permute-done | bytes 184352 | tf_op jit(solution)/shard_map/ppermute | solution.py:182
  26.1 7.3 %collective-permute-start.3 = (bf16[168,256]{1,0:T(8,128)(2,1)S(1)}, bf16[168,256]{1,0:T(8,128)(2,1)S(1)}, u32[]{:S(2)}, u32[]{:S(2)}) collective-permute-start(bf16[168,256]{1,0:T(8,128)(2,1)S(1)} %slice.9), channel_id=1, source_target_pairs={{0,6},{2,0},{4,2},{6,4},{1,7},{3,1},{5,3},{7,5},{8,14},{10,8},{12,... | collective-permute-start | bytes 258056 | tf_op jit(solution)/shard_map/ppermute | solution.py:182
  33.4 3.6 %collective-permute-done.refs_1_ = bf16[360,256]{1,0:T(8,128)(2,1)S(1)} collective-permute-done((bf16[360,256]{1,0:T(8,128)(2,1)}, bf16[360,256]{1,0:T(8,128)(2,1)S(1)}, u32[]{:S(2)}, u32[]{:S(2)}) %collective-permute-start) | collective-permute-done | bytes 184352 | tf_op jit(solution)/shard_map/ppermute | solution.py:182
  37.0 2.1 %collective-permute-start.2 = (bf16[192,256]{1,0:T(8,128)(2,1)S(1)}, bf16[192,256]{1,0:T(8,128)(2,1)S(1)}, u32[]{:S(2)}, u32[]{:S(2)}) collective-permute-start(bf16[192,256]{1,0:T(8,128)(2,1)S(1)} %slice.8), channel_id=1, source_target_pairs={{0,2},{2,4},{4,6},{6,0},{1,3},{3,5},{5,7},{7,1},{8,10},{10,12},{12... | collective-permute-start | bytes 294920 | tf_op jit(solution)/shard_map/ppermute | solution.py:182
  39.1 1.9 %collective-permute-start.6 = (bf16[360,256]{1,0:T(8,128)(2,1)S(1)}, bf16[360,256]{1,0:T(8,128)(2,1)S(1)}, u32[]{:S(2)}, u32[]{:S(2)}) collective-permute-start(bf16[360,256]{1,0:T(8,128)(2,1)S(1)} %collective-permute-done.1.refs_2_), channel_id=1, source_target_pairs={{0,1},{1,0},{2,3},{3,2},{4,5},{5,4},{6,7},{7,6},{8,9},{9,8},{10,11... | collective-permute-start | bytes 552968 | tf_op jit(solution)/shard_map/ppermute | solution.py:182
  41.0 2.4 %collective-permute-start.5 = (bf16[360,256]{1,0:T(8,128)(2,1)S(1)}, bf16[360,256]{1,0:T(8,128)(2,1)S(1)}, u32[]{:S(2)}, u32[]{:S(2)}) collective-permute-start(bf16[360,256]{1,0:T(8,128)(2,1)S(1)} %collective-permute-done.refs_1_), channel_id=1, source_target_pairs={{0,1},{1,0},{2,3},{3,2},{4,5},{5,4},{6,7},{7,6},{8,9},{9,8},{10,11... | collective-permute-start | bytes 552968 | tf_op jit(solution)/shard_map/ppermute | solution.py:182
  44.9 1.9 %collective-permute-start.8 = (bf16[168,256]{1,0:T(8,128)(2,1)S(1)}, bf16[168,256]{1,0:T(8,128)(2,1)S(1)}, u32[]{:S(2)}, u32[]{:S(2)}) collective-permute-start(bf16[168,256]{1,0:T(8,128)(2,1)S(1)} %collective-permute-done.3.refs_4_), channel_id=1, source_target_pairs={{0,1},{1,0},{2,3},{3,2},{4,5},{5,4},{6,7},{7,6},{8,9},{9,8},{10,11... | collective-permute-start | bytes 258056 | tf_op jit(solution)/shard_map/ppermute | solution.py:182
  46.8 2.4 %collective-permute-done.2.refs_3_ = bf16[192,256]{1,0:T(8,128)(2,1)S(1)} collective-permute-done((bf16[192,256]{1,0:T(8,128)(2,1)S(1)}, bf16[192,256]{1,0:T(8,128)(2,1)S(1)}, u32[]{:S(2)}, u32[]{:S(2)}) %collective-permute-start.2) | collective-permute-done | bytes 98336 | tf_op jit(solution)/shard_map/ppermute | solution.py:182
  49.2 1.9 %collective-permute-start.7 = (bf16[192,256]{1,0:T(8,128)(2,1)S(1)}, bf16[192,256]{1,0:T(8,128)(2,1)S(1)}, u32[]{:S(2)}, u32[]{:S(2)}) collective-permute-start(bf16[192,256]{1,0:T(8,128)(2,1)S(1)} %collective-permute-done.2.refs_3_), channel_id=1, source_target_pairs={{0,1},{1,0},{2,3},{3,2},{4,5},{5,4},{6,7},{7,6},{8,9},{9,8},{10,11... | collective-permute-start | bytes 294920 | tf_op jit(solution)/shard_map/ppermute | solution.py:182
  52.4 1.5 %copy-done = bf16[1,192,1,5120]{3,1,2,0:T(8,128)(2,1)S(1)} copy-done((bf16[1,192,1,5120]{3,1,2,0:T(8,128)(2,1)S(1)}, bf16[1,192,1,5120]{3,1,2,0:T(8,128)(2,1)}, u32[]{:S(2)}) %copy-start) | copy-done | bytes 1966104
  54.8 3.1 %shard_map.51 = (bf16[192,5120]{1,0:T(8,128)(2,1)S(1)}, bf16[72,192]{1,0:T(8,128)(2,1)S(1)}, bf16[72,192]{1,0:T(8,128)(2,1)S(1)}) custom-call(s32[2]{0:T(128)S(1)} %pad_add_fusion.pos_ref, bf16[360,256]{1,0:T(8,128)(2,1)S(1)} %copy-done.3, bf16[360,256]{1,0:T(8,128)(2,1)S(1)} %collective-permute-done.refs_1_, ...), custom_call_target="tpu_custom_call" | custom-call | tf_op jit(solution)/shard_map/pallas_call | solution.py:108
  58.0 1.3 copy-done.2
  59.2 5.3 %all-to-all-start = ((bf16[4,48,5120]{2,1,0:T(8,128)(2,1)}), bf16[4,48,5120]{2,1,0:T(8,128)(2,1)}, u32[]{:S(2)}, u32[]{:S(2)}) async-start(bf16[4,48,5120]{2,1,0:T(8,128)(2,1)} %bitcast.10), calls=%async_computation | async-start | bytes 3932160 | tf_op jit(solution)/shard_map/all_to_all | solution.py:186
  64.6 1.9 %collective-permute-start.10 = (bf16[192,5120]{1,0:T(8,128)(2,1)S(1)}, bf16[192,5120]{1,0:T(8,128)(2,1)}, u32[]{:S(2)}, u32[]{:S(2)}) collective-permute-start(bf16[192,5120]{1,0:T(8,128)(2,1)S(1)} %bitcast.8), channel_id=1, source_target_pairs={{0,1},{1,0},{2,3},{3,2},{4,5},{5,4},{6,7},{7,6},{8,9},{9,8},{10,11... | collective-permute-start | bytes 5898248 | tf_op jit(solution)/shard_map/ppermute | solution.py:182
  66.5 23.6 %all-to-all-done = bf16[4,48,5120]{2,1,0:T(8,128)(2,1)} async-done(((bf16[4,48,5120]{2,1,0:T(8,128)(2,1)}), bf16[4,48,5120]{2,1,0:T(8,128)(2,1)}, u32[]{:S(2)}, u32[]{:S(2)}) %all-to-all-start) | async-done | bytes 1966112 | tf_op jit(solution)/shard_map/all_to_all | solution.py:186
  90.1 2.8 %reduce_sum.36 = bf16[48,5120]{1,0:T(8,128)(2,1)} reduce(bf16[4,48,5120]{2,1,0:T(8,128)(2,1)} %all-to-all-done, bf16[]{:T(256)} %constant.86.clone.1), dimensions={0}, to_apply=%region_0.1 | reduce | flops 737280 | bytes 2457602 | tf_op jit(solution)/shard_map/reduce_sum | solution.py:187
  92.9 4.2 %all-to-all-start.1 = ((bf16[3,16,5120]{2,1,0:T(8,128)(2,1)}), bf16[3,16,5120]{2,1,0:T(8,128)(2,1)S(1)}, u32[]{:S(2)}, u32[]{:S(2)}) async-start(bf16[3,16,5120]{2,1,0:T(8,128)(2,1)} %bitcast.5), calls=%async_computation.1 | async-start | bytes 983040 | tf_op jit(solution)/shard_map/all_to_all | solution.py:186
  97.1 1.9 %collective-permute-start.9 = (bf16[72,192]{1,0:T(8,128)(2,1)S(1)}, bf16[72,192]{1,0:T(8,128)(2,1)S(1)}, u32[]{:S(2)}, u32[]{:S(2)}) collective-permute-start(bf16[72,192]{1,0:T(8,128)(2,1)S(1)} %get-tuple-element.13), channel_id=1, source_target_pairs={{0,1},{1,0},{2,3},{3,2},{4,5},{5,4},{6,7},{7,6},{8,9},{9,8},{10,11... | collective-permute-start | bytes 82952 | tf_op jit(solution)/shard_map/ppermute | solution.py:182
  100.2 2.8 %shard_map.52 = (f32[360,256]{1,0:T(8,128)S(1)}, f32[360,256]{1,0:T(8,128)S(1)}, f32[360,256]{1,0:T(8,128)S(1)}, bf16[192,256]{1,0:T(8,128)(2,1)S(1)}, bf16[168,256]{1,0:T(8,128)(2,1)S(1)}) custom-call(s32[2]{0:T(128)S(1)} %pad_add_fusion.pos_ref, bf16[72,192]{1,0:T(8,128)(2,1)S(1)} %get-tuple-element.12.mine_ref, ...), custom_call_target="tpu_custom_call" | custom-call | tf_op jit(solution)/shard_map/pallas_call | solution.py:147
  104.4 2.9 %collective-permute-start.11 = (bf16[192,256]{1,0:T(8,128)(2,1)S(1)}, bf16[192,256]{1,0:T(8,128)(2,1)S(1)}, u32[]{:S(2)}, u32[]{:S(2)}) collective-permute-start(bf16[192,256]{1,0:T(8,128)(2,1)S(1)} %get-tuple-element.17), channel_id=1, source_target_pairs={{0,2},{2,4},{4,6},{6,0},{1,3},{3,5},{5,7},{7,1},{8,10},{10,12},{12... | collective-permute-start | bytes 294920 | tf_op jit(solution)/shard_map/ppermute | solution.py:182
  107.3 6.0 %collective-permute-start.12 = (bf16[168,256]{1,0:T(8,128)(2,1)S(1)}, bf16[168,256]{1,0:T(8,128)(2,1)S(1)}, u32[]{:S(2)}, u32[]{:S(2)}) collective-permute-start(bf16[168,256]{1,0:T(8,128)(2,1)S(1)} %get-tuple-element.18), channel_id=1, source_target_pairs={{0,6},{2,0},{4,2},{6,4},{1,7},{3,1},{5,3},{7,5},{8,14},{10,8},{12,... | collective-permute-start | bytes 258056 | tf_op jit(solution)/shard_map/ppermute | solution.py:182
  113.3 5.7 %collective-permute-done.12.far_b = bf16[168,256]{1,0:T(8,128)(2,1)S(1)} collective-permute-done((bf16[168,256]{1,0:T(8,128)(2,1)S(1)}, bf16[168,256]{1,0:T(8,128)(2,1)S(1)}, u32[]{:S(2)}, u32[]{:S(2)}) %collective-permute-start.12) | collective-permute-done | bytes 86048 | tf_op jit(solution)/shard_map/ppermute | solution.py:182
  119.6 1.9 %shard_map.53 = (bf16[360,256]{1,0:T(8,128)(2,1)}, bf16[360,256]{1,0:T(8,128)(2,1)}) custom-call(f32[360,256]{1,0:T(8,128)} %copy-done.4, f32[360,256]{1,0:T(8,128)} %copy-done.5, bf16[192,256]{1,0:T(8,128)(2,1)} %copy-done.6, bf16[168,256]{1,0:T(8,128)(2,1)} %copy-done.7), custom_call_target="tpu_custom_call" | custom-call | tf_op jit(solution)/shard_map/pallas_call | solution.py:172
  121.5 5.1 %collective-permute-start.13 = (bf16[360,256]{1,0:T(8,128)(2,1)}, bf16[360,256]{1,0:T(8,128)(2,1)S(1)}, u32[]{:S(2)}, u32[]{:S(2)}) collective-permute-start(bf16[360,256]{1,0:T(8,128)(2,1)} %get-tuple-element.19), channel_id=1, source_target_pairs={{0,2},{2,4},{4,6},{6,0},{1,3},{3,5},{5,7},{7,1},{8,10},{10,12},{12... | collective-permute-start | bytes 552968 | tf_op jit(solution)/shard_map/ppermute | solution.py:182
  126.6 3.8 %collective-permute-start.14 = (bf16[360,256]{1,0:T(8,128)(2,1)}, bf16[360,256]{1,0:T(8,128)(2,1)S(1)}, u32[]{:S(2)}, u32[]{:S(2)}) collective-permute-start(bf16[360,256]{1,0:T(8,128)(2,1)} %get-tuple-element.20), channel_id=1, source_target_pairs={{0,6},{2,0},{4,2},{6,4},{1,7},{3,1},{5,3},{7,5},{8,14},{10,8},{12,... | collective-permute-start | bytes 552968 | tf_op jit(solution)/shard_map/ppermute | solution.py:182
  131.2 7.3 %all-to-all-start.2 = ((bf16[8,2,5120]{2,1,0:T(2,128)(2,1)}), bf16[8,2,5120]{2,1,0:T(2,128)(2,1)S(1)}, u32[]{:S(2)}, u32[]{:S(2)}) async-start(bf16[8,2,5120]{2,1,0:T(2,128)(2,1)} %reshape.26), calls=%async_computation.2 | async-start | bytes 327680 | tf_op jit(solution)/shard_map/all_to_all | solution.py:186
  138.6 3.0 %collective-permute-done.14 = bf16[360,256]{1,0:T(8,128)(2,1)S(1)} collective-permute-done((bf16[360,256]{1,0:T(8,128)(2,1)}, bf16[360,256]{1,0:T(8,128)(2,1)S(1)}, u32[]{:S(2)}, u32[]{:S(2)}) %collective-permute-start.14) | collective-permute-done | bytes 184352 | tf_op jit(solution)/shard_map/ppermute | solution.py:182
  142.4 5.6 %all-to-all-done.2 = bf16[8,2,5120]{2,1,0:T(2,128)(2,1)S(1)} async-done(((bf16[8,2,5120]{2,1,0:T(2,128)(2,1)}), bf16[8,2,5120]{2,1,0:T(2,128)(2,1)S(1)}, u32[]{:S(2)}, u32[]{:S(2)}) %all-to-all-start.2) | async-done | bytes 163872 | tf_op jit(solution)/shard_map/all_to_all | solution.py:186
  (40 shorter events, 9.4 us)
Async XLA Ops:
  2.4 48.7 %collective-permute-start.4 = (bf16[360,256]{1,0:T(8,128)(2,1)}, bf16[360,256]{1,0:T(8,128)(2,1)S(1)}, u32[]{:S(2)}, u32[]{:S(2)}) collective-permute-start(bf16[360,256]{1,0:T(8,128)(2,1)} %shard_map.50.refs_0_), channel_id=1, source_target_pairs={{0,1},{1,0},{2,3},{3,2},{4,5},{5,4},{6,7},{7,6},{8,9},{9,8},{10,11... | collective-permute-start | bytes 552968 | tf_op jit(solution)/shard_map/ppermute | solution.py:182
  4.4 21.7 %collective-permute-start.1 = (bf16[360,256]{1,0:T(8,128)(2,1)}, bf16[360,256]{1,0:T(8,128)(2,1)S(1)}, u32[]{:S(2)}, u32[]{:S(2)}) collective-permute-start(bf16[360,256]{1,0:T(8,128)(2,1)} %shard_map.50.refs_0_), channel_id=1, source_target_pairs={{0,6},{2,0},{4,2},{6,4},{1,7},{3,1},{5,3},{7,5},{8,14},{10,8},{12,... | collective-permute-start | bytes 552968 | tf_op jit(solution)/shard_map/ppermute | solution.py:182
  17.1 19.8 %collective-permute-start = (bf16[360,256]{1,0:T(8,128)(2,1)}, bf16[360,256]{1,0:T(8,128)(2,1)S(1)}, u32[]{:S(2)}, u32[]{:S(2)}) collective-permute-start(bf16[360,256]{1,0:T(8,128)(2,1)} %shard_map.50.refs_0_), channel_id=1, source_target_pairs={{0,2},{2,4},{4,6},{6,0},{1,3},{3,5},{5,7},{7,1},{8,10},{10,12},{12... | collective-permute-start | bytes 552968 | tf_op jit(solution)/shard_map/ppermute | solution.py:182
  26.1 18.8 %collective-permute-start.3 = (bf16[168,256]{1,0:T(8,128)(2,1)S(1)}, bf16[168,256]{1,0:T(8,128)(2,1)S(1)}, u32[]{:S(2)}, u32[]{:S(2)}) collective-permute-start(bf16[168,256]{1,0:T(8,128)(2,1)S(1)} %slice.9), channel_id=1, source_target_pairs={{0,6},{2,0},{4,2},{6,4},{1,7},{3,1},{5,3},{7,5},{8,14},{10,8},{12,... | collective-permute-start | bytes 258056 | tf_op jit(solution)/shard_map/ppermute | solution.py:182
  37.0 12.2 %collective-permute-start.2 = (bf16[192,256]{1,0:T(8,128)(2,1)S(1)}, bf16[192,256]{1,0:T(8,128)(2,1)S(1)}, u32[]{:S(2)}, u32[]{:S(2)}) collective-permute-start(bf16[192,256]{1,0:T(8,128)(2,1)S(1)} %slice.8), channel_id=1, source_target_pairs={{0,2},{2,4},{4,6},{6,0},{1,3},{3,5},{5,7},{7,1},{8,10},{10,12},{12... | collective-permute-start | bytes 294920 | tf_op jit(solution)/shard_map/ppermute | solution.py:182
  39.1 12.1 %collective-permute-start.6 = (bf16[360,256]{1,0:T(8,128)(2,1)S(1)}, bf16[360,256]{1,0:T(8,128)(2,1)S(1)}, u32[]{:S(2)}, u32[]{:S(2)}) collective-permute-start(bf16[360,256]{1,0:T(8,128)(2,1)S(1)} %collective-permute-done.1.refs_2_), channel_id=1, source_target_pairs={{0,1},{1,0},{2,3},{3,2},{4,5},{5,4},{6,7},{7,6},{8,9},{9,8},{10,11... | collective-permute-start | bytes 552968 | tf_op jit(solution)/shard_map/ppermute | solution.py:182
  41.0 10.2 %collective-permute-start.5 = (bf16[360,256]{1,0:T(8,128)(2,1)S(1)}, bf16[360,256]{1,0:T(8,128)(2,1)S(1)}, u32[]{:S(2)}, u32[]{:S(2)}) collective-permute-start(bf16[360,256]{1,0:T(8,128)(2,1)S(1)} %collective-permute-done.refs_1_), channel_id=1, source_target_pairs={{0,1},{1,0},{2,3},{3,2},{4,5},{5,4},{6,7},{7,6},{8,9},{9,8},{10,11... | collective-permute-start | bytes 552968 | tf_op jit(solution)/shard_map/ppermute | solution.py:182
  44.9 6.3 %collective-permute-start.8 = (bf16[168,256]{1,0:T(8,128)(2,1)S(1)}, bf16[168,256]{1,0:T(8,128)(2,1)S(1)}, u32[]{:S(2)}, u32[]{:S(2)}) collective-permute-start(bf16[168,256]{1,0:T(8,128)(2,1)S(1)} %collective-permute-done.3.refs_4_), channel_id=1, source_target_pairs={{0,1},{1,0},{2,3},{3,2},{4,5},{5,4},{6,7},{7,6},{8,9},{9,8},{10,11... | collective-permute-start | bytes 258056 | tf_op jit(solution)/shard_map/ppermute | solution.py:182
  49.2 3.2 %collective-permute-start.7 = (bf16[192,256]{1,0:T(8,128)(2,1)S(1)}, bf16[192,256]{1,0:T(8,128)(2,1)S(1)}, u32[]{:S(2)}, u32[]{:S(2)}) collective-permute-start(bf16[192,256]{1,0:T(8,128)(2,1)S(1)} %collective-permute-done.2.refs_3_), channel_id=1, source_target_pairs={{0,1},{1,0},{2,3},{3,2},{4,5},{5,4},{6,7},{7,6},{8,9},{9,8},{10,11... | collective-permute-start | bytes 294920 | tf_op jit(solution)/shard_map/ppermute | solution.py:182
  52.4 1.5 %copy-start = (bf16[1,192,1,5120]{3,1,2,0:T(8,128)(2,1)S(1)}, bf16[1,192,1,5120]{3,1,2,0:T(8,128)(2,1)}, u32[]{:S(2)}) copy-start(bf16[1,192,1,5120]{3,1,2,0:T(8,128)(2,1)} %param.3) | copy-start | bytes 5898244
  53.9 0.9 copy-start.3
  57.9 1.3 copy-start.2
  59.2 5.4 %copy-start.1 = (bf16[1,192,1,5120]{3,1,2,0:T(8,128)(2,1)S(1)}, bf16[1,192,1,5120]{3,1,2,0:T(8,128)(2,1)}, u32[]{:S(2)}) copy-start(bf16[1,192,1,5120]{3,1,2,0:T(8,128)(2,1)} %param.3) | copy-start | bytes 5898244
  59.2 30.8 %all-to-all-start = ((bf16[4,48,5120]{2,1,0:T(8,128)(2,1)}), bf16[4,48,5120]{2,1,0:T(8,128)(2,1)}, u32[]{:S(2)}, u32[]{:S(2)}) async-start(bf16[4,48,5120]{2,1,0:T(8,128)(2,1)} %bitcast.10), calls=%async_computation | async-start | bytes 3932160 | tf_op jit(solution)/shard_map/all_to_all | solution.py:186
  64.6 35.6 %collective-permute-start.10 = (bf16[192,5120]{1,0:T(8,128)(2,1)S(1)}, bf16[192,5120]{1,0:T(8,128)(2,1)}, u32[]{:S(2)}, u32[]{:S(2)}) collective-permute-start(bf16[192,5120]{1,0:T(8,128)(2,1)S(1)} %bitcast.8), channel_id=1, source_target_pairs={{0,1},{1,0},{2,3},{3,2},{4,5},{5,4},{6,7},{7,6},{8,9},{9,8},{10,11... | collective-permute-start | bytes 5898248 | tf_op jit(solution)/shard_map/ppermute | solution.py:182
  92.9 37.5 %all-to-all-start.1 = ((bf16[3,16,5120]{2,1,0:T(8,128)(2,1)}), bf16[3,16,5120]{2,1,0:T(8,128)(2,1)S(1)}, u32[]{:S(2)}, u32[]{:S(2)}) async-start(bf16[3,16,5120]{2,1,0:T(8,128)(2,1)} %bitcast.5), calls=%async_computation.1 | async-start | bytes 983040 | tf_op jit(solution)/shard_map/all_to_all | solution.py:186
  97.1 3.1 %collective-permute-start.9 = (bf16[72,192]{1,0:T(8,128)(2,1)S(1)}, bf16[72,192]{1,0:T(8,128)(2,1)S(1)}, u32[]{:S(2)}, u32[]{:S(2)}) collective-permute-start(bf16[72,192]{1,0:T(8,128)(2,1)S(1)} %get-tuple-element.13), channel_id=1, source_target_pairs={{0,1},{1,0},{2,3},{3,2},{4,5},{5,4},{6,7},{7,6},{8,9},{9,8},{10,11... | collective-permute-start | bytes 82952 | tf_op jit(solution)/shard_map/ppermute | solution.py:182
  103.0 0.7 copy-start.4
  103.7 0.7 copy-start.5
  104.4 14.5 %collective-permute-start.11 = (bf16[192,256]{1,0:T(8,128)(2,1)S(1)}, bf16[192,256]{1,0:T(8,128)(2,1)S(1)}, u32[]{:S(2)}, u32[]{:S(2)}) collective-permute-start(bf16[192,256]{1,0:T(8,128)(2,1)S(1)} %get-tuple-element.17), channel_id=1, source_target_pairs={{0,2},{2,4},{4,6},{6,0},{1,3},{3,5},{5,7},{7,1},{8,10},{10,12},{12... | collective-permute-start | bytes 294920 | tf_op jit(solution)/shard_map/ppermute | solution.py:182
  107.3 11.7 %collective-permute-start.12 = (bf16[168,256]{1,0:T(8,128)(2,1)S(1)}, bf16[168,256]{1,0:T(8,128)(2,1)S(1)}, u32[]{:S(2)}, u32[]{:S(2)}) collective-permute-start(bf16[168,256]{1,0:T(8,128)(2,1)S(1)} %get-tuple-element.18), channel_id=1, source_target_pairs={{0,6},{2,0},{4,2},{6,4},{1,7},{3,1},{5,3},{7,5},{8,14},{10,8},{12,... | collective-permute-start | bytes 258056 | tf_op jit(solution)/shard_map/ppermute | solution.py:182
  119.0 0.6 copy-start.7
  119.0 0.7 copy-start.6
  121.5 17.0 %collective-permute-start.13 = (bf16[360,256]{1,0:T(8,128)(2,1)}, bf16[360,256]{1,0:T(8,128)(2,1)S(1)}, u32[]{:S(2)}, u32[]{:S(2)}) collective-permute-start(bf16[360,256]{1,0:T(8,128)(2,1)} %get-tuple-element.19), channel_id=1, source_target_pairs={{0,2},{2,4},{4,6},{6,0},{1,3},{3,5},{5,7},{7,1},{8,10},{10,12},{12... | collective-permute-start | bytes 552968 | tf_op jit(solution)/shard_map/ppermute | solution.py:182
  126.6 15.0 %collective-permute-start.14 = (bf16[360,256]{1,0:T(8,128)(2,1)}, bf16[360,256]{1,0:T(8,128)(2,1)S(1)}, u32[]{:S(2)}, u32[]{:S(2)}) collective-permute-start(bf16[360,256]{1,0:T(8,128)(2,1)} %get-tuple-element.20), channel_id=1, source_target_pairs={{0,6},{2,0},{4,2},{6,4},{1,7},{3,1},{5,3},{7,5},{8,14},{10,8},{12,... | collective-permute-start | bytes 552968 | tf_op jit(solution)/shard_map/ppermute | solution.py:182
  131.2 16.8 %all-to-all-start.2 = ((bf16[8,2,5120]{2,1,0:T(2,128)(2,1)}), bf16[8,2,5120]{2,1,0:T(2,128)(2,1)S(1)}, u32[]{:S(2)}, u32[]{:S(2)}) async-start(bf16[8,2,5120]{2,1,0:T(2,128)(2,1)} %reshape.26), calls=%async_computation.2 | async-start | bytes 327680 | tf_op jit(solution)/shard_map/all_to_all | solution.py:186

commit v2 on v1

v2 whole, which is shorter than its diff:
```python
import functools
import math

import jax
import jax.numpy as jnp
from jax import lax
from jax.experimental import pallas as pl
from jax.experimental.pallas import tpu as pltpu
from jax.sharding import Mesh, PartitionSpec as P

EPS = 1e-06
LANES = 128
INTER = ("yh", "yl", "zl", "x")
FIRST = ("x", "yl")
SECOND = ("yh", "zl")
F32 = jnp.float32
BF16 = jnp.bfloat16
VMEM = pl.BlockSpec(memory_space=pltpu.VMEM)
HBM = pl.BlockSpec(memory_space=pltpu.HBM)
SPANS = 5
PARAMS = pltpu.CompilerParams(vmem_limit_bytes=40 << 20)


def requantized(blocks):
    scales = (jnp.max(jnp.abs(blocks), axis=-1, keepdims=True) + EPS).astype(BF16).astype(F32)
    values = (blocks / scales).astype(BF16).astype(F32)
    return values * scales


def quantize_kernel(w_ref, out_ref):
    out_ref[...] = requantized(w_ref[...]).astype(BF16)


def quantize_weight(weight):
    return pl.pallas_call(
        quantize_kernel,
        out_shape=jax.ShapeDtypeStruct(weight.shape, BF16),
        in_specs=[VMEM],
        out_specs=VMEM,
    )(weight)


def quotient(number, by, count):
    return sum((number >= by * k).astype(jnp.int32) for k in range(1, count))


def permutation(tokens, held, wanted):
    new = lax.broadcasted_iota(jnp.int32, (tokens, tokens), 0)
    old = lax.broadcasted_iota(jnp.int32, (tokens, tokens), 1)
    sizes = dict(held)
    own = tokens // math.prod(sizes.values())
    index, rest, stride = {}, new, tokens
    for axis in wanted:
        stride //= sizes[axis]
        index[axis] = quotient(rest, stride, sizes[axis])
        rest = rest - index[axis] * stride
    source = jnp.zeros_like(new)
    for axis, size in held:
        source = source * size + index[axis]
    source = source * own + rest
    return (source == old).astype(F32).astype(BF16)


def gate_kernel(orders, pos_ref, wa_ref, wb_ref, x_hbm, c_ref, part_hbm, keep_ref, send_ref, *scratch):
    w32, wmat, x_ref, part_ref, sem_in, sem_out = scratch
    core = pos_ref[1]
    span = x_ref.shape[1] // SPANS
    spans = [slice(i * span, (i + 1) * span) for i in range(SPANS)]
    loads = [
        pltpu.make_async_copy(x_hbm.at[:, at], x_ref.at[:, at], sem_in.at[i])
        for i, at in enumerate(spans)
    ]
    stores = [
        pltpu.make_async_copy(part_ref.at[:, at], part_hbm.at[:, at], sem_out.at[i])
        for i, at in enumerate(spans)
    ]
    for load in loads:
        load.start()
    rows = wmat.shape[0]
    chunk, block = wa_ref.shape
    per_row = w32.shape[1] // rows
    lanes = w32.shape[2]
    halves = block // lanes
    for i, w_ref in enumerate((wa_ref, wb_ref)):
        for k in range(halves):
            half = w_ref[:, k * lanes : (k + 1) * lanes].astype(F32)
            w32[k, i * chunk : (i + 1) * chunk] = half
    proj = jnp.zeros((rows, x_ref.shape[0]), F32)
    for b in range(per_row):
        columns = slice(b * block, (b + 1) * block)
        if b * block % span == 0:
            loads[b * block // span].wait()
        w = jnp.concatenate(
            [w32[k, pl.ds(b, rows, stride=per_row), :] for k in range(halves)], axis=1
        ).astype(BF16)
        wmat[:, columns] = w
        proj += lax.dot_general(
            w, x_ref[:, columns], (((1,), (1,)), ((), ())), preferred_element_type=F32
        )
    quarter = rows // 4
    eighth = quarter // 2
    cot = c_ref[...].astype(F32)
    low = jnp.concatenate([cot[:eighth], cot[quarter : quarter + eighth]], axis=0)
    high = jnp.concatenate([cot[eighth:quarter], cot[quarter + eighth :]], axis=0)
    pre = []
    for dc in range(2):
        base = dc * 2 * quarter
        gate = proj[base : base + quarter]
        upper = proj[base + quarter : base + 2 * quarter]
        c = jnp.where(core == dc, low, high)
        sig = jax.nn.sigmoid(gate)
        pre.append(c * upper * sig * (1.0 + gate * (1.0 - sig)))
        pre.append(c * gate * sig)
    keep = jnp.concatenate(pre[:2], axis=0)
    send = jnp.concatenate(pre[2:], axis=0)
    keep_ref[...] = keep.astype(BF16)
    send_ref[...] = send.astype(BF16)
    pre = jnp.concatenate([keep, send], axis=0).astype(BF16)
    pre = lax.dot_general(
        permutation(x_ref.shape[0], *orders),
        pre,
        (((1,), (1,)), ((), ())),
        preferred_element_type=F32,
    ).astype(BF16)
    for b in range(per_row):
        columns = slice(b * block, (b + 1) * block)
        part_ref[:, columns] = jnp.dot(
            pre, wmat[:, columns], preferred_element_type=F32
        ).astype(BF16)
        if (b + 1) * block % span == 0:
            stores[b * block // span].start()
    for store in stores:
        store.wait()


def gate_part(orders, pos, w_mine, w_other, x, cot):
    tokens, width = x.shape
    rows = 2 * cot.shape[0]
    block = w_mine.shape[1]
    return pl.pallas_call(
        functools.partial(gate_kernel, orders),
        out_shape=(
            jax.ShapeDtypeStruct((tokens, width), BF16),
            jax.ShapeDtypeStruct((rows // 2, tokens), BF16),
            jax.ShapeDtypeStruct((rows // 2, tokens), BF16),
        ),
        in_specs=[pl.BlockSpec(memory_space=pltpu.SMEM), VMEM, VMEM, HBM, VMEM],
        out_specs=(HBM, VMEM, VMEM),
        scratch_shapes=[
            pltpu.VMEM((block // LANES, 2 * w_mine.shape[0], LANES), F32),
            pltpu.VMEM((rows, width), BF16),
            pltpu.VMEM((tokens, width), BF16),
            pltpu.VMEM((tokens, width), BF16),
            pltpu.SemaphoreType.DMA((SPANS,)),
            pltpu.SemaphoreType.DMA((SPANS,)),
        ],
        compiler_params=pltpu.CompilerParams(vmem_limit_bytes=61_600_000),
    )(pos, w_mine, w_other, x, cot)


def weight_grad_kernel(steps, pos_ref, mine_ref, got_ref, x_ref, xo_ref, *refs):
    outs, g32 = refs[: len(steps)], refs[len(steps)]
    zh = pos_ref[0]
    rows = mine_ref.shape[0]
    chunk, block = outs[0].shape
    n_z = len(steps)
    per_row = n_z * chunk // rows
    lanes = g32.shape[2]
    for b in range(per_row):
        columns = slice(b * block, (b + 1) * block)
        local = requantized(
            jnp.dot(mine_ref[...], x_ref[:, columns], preferred_element_type=F32)
        ) + requantized(jnp.dot(got_ref[...], xo_ref[:, columns], preferred_element_type=F32))
        for k in range(block // lanes):
            g32[k, pl.ds(b, rows, stride=per_row), :] = local[:, k * lanes : (k + 1) * lanes]
    for out, dz in zip(outs, steps):
        at = pl.multiple_of(lax.rem(zh + dz, n_z) * chunk, 8)
        for k in range(block // lanes):
            piece = g32[k, pl.ds(at, chunk), :]
            out[:, k * lanes : (k + 1) * lanes] = piece.astype(out.dtype)


def weight_grad_part(steps, pos, mine, got, x, x_other, chunk, block):
    return pl.pallas_call(
        functools.partial(weight_grad_kernel, steps),
        out_shape=[
            jax.ShapeDtypeStruct((chunk, block), BF16 if dz else F32) for dz in steps
        ],
        in_specs=[pl.BlockSpec(memory_space=pltpu.SMEM)] + [VMEM] * 4,
        out_specs=[VMEM] * len(steps),
        scratch_shapes=[pltpu.VMEM((block // LANES, len(steps) * chunk, LANES), F32)],
        compiler_params=PARAMS,
    )(pos, mine, got, x, x_other)


def total_kernel(scale, total_ref, *refs):
    total = total_ref[...]
    for piece in refs[:-1]:
        total = total + piece[...].astype(F32)
    refs[-1][...] = total * scale


def scaled_total(scale, total, pieces):
    return pl.pallas_call(
        functools.partial(total_kernel, scale),
        out_shape=jax.ShapeDtypeStruct(total.shape, F32),
        in_specs=[VMEM] * (1 + len(pieces)),
        out_specs=VMEM,
        cost_estimate=pl.CostEstimate(flops=10**11, bytes_accessed=0, transcendentals=0),
        compiler_params=PARAMS,
    )(total, *pieces)


def step(array, axis, by):
    n = lax.axis_size(axis)
    return lax.ppermute(array, axis, [(i, (i + by) % n) for i in range(n)])


def swapped(array):
    return lax.ppermute(array, "c", [(0, 1), (1, 0)])


def summed_pieces(pieces):
    return jnp.sum(pieces.astype(F32), axis=0).astype(BF16)


def spread(array, axes):
    return lax.all_to_all(array, axes, split_axis=0, concat_axis=0, tiled=True)


def body(activations, hidden_cot, weight):
    tok = activations.shape[1] * activations.shape[2]
    width = activations.shape[3]
    hidden = hidden_cot.shape[3]
    n_z = lax.axis_size("zh")
    x = activations.reshape(tok, width)
    cot = hidden_cot.reshape(tok, hidden).T
    pos = jnp.stack([lax.axis_index("zh"), lax.axis_index("c")]).astype(jnp.int32)
    chunk, block = weight.shape

    own = quantize_weight(weight)
    w_mine = lax.all_gather(own, "zh", axis=0, tiled=True)
    w_mine, x_late = lax.optimization_barrier((w_mine, x))
    w_other = swapped(w_mine)
    x_other = swapped(x_late)
    held = tuple((axis, lax.axis_size(axis)) for axis in INTER)
    part, keep, send = gate_part((held, FIRST + SECOND), pos, w_mine, w_other, x, cot)

    first = math.prod(lax.axis_size(axis) for axis in FIRST)
    second = math.prod(lax.axis_size(axis) for axis in SECOND)
    rows = spread(part.reshape(first, -1, width), FIRST)
    got = swapped(send)
    steps = (0, n_z // 2) + tuple(dz for dz in range(1, n_z) if dz != n_z // 2)
    total, *chunks = weight_grad_part(steps, pos, keep, got, x, x_other, chunk, block)
    rows, _ = lax.optimization_barrier((rows, chunks))
    arrived = [step(piece, "zh", dz) for piece, dz in zip(chunks, steps[1:])]
    rows = summed_pieces(rows)
    rows = spread(rows.reshape(second, -1, width), SECOND)
    input_grad = summed_pieces(rows).reshape(1, -1, activations.shape[2], width)
    scale = 1.0 / math.sqrt(tok * n_z * lax.axis_size("c"))
    weight_grad = scaled_total(scale, total, arrived)
    return (weight_grad, input_grad)


def solution(mesh):
    fine = Mesh(mesh.devices.reshape(4, 2, 3, 4, 4, 2), INTER + ("zh", "c"))
    return jax.shard_map(
        body,
        mesh=fine,
        in_specs=(
            P(("zh", "c"), None, None, None),
            P(("zh", "c"), None, None, INTER),
            P(INTER + ("zh", "c"), None),
        ),
        out_specs=(P(INTER + ("zh", "c"), None), P(("zh", "c"), INTER, None, None)),
        check_vma=False,
    )
```

time: 150 us -> 106 us (0.71)
  the two profiles are of different devices: /device:TPU:128 before, /device:TPU:1 now
where the time goes in v2:
time: 106 us
  starting transfers between devices  37.5 us (35%)
  blocking collectives  34.3 us (32%)
  waiting for transfers between devices  17.2 us (16%)
  Pallas kernels  10.9 us (10%)
  other arithmetic  3.28 us (3%)
  local copies, waits for them, and re-layouts  1.68 us (2%)
    all_gather x1, blocking collectives, body(): w_mine = lax.all_gather(own, 'zh', axis=0, tiled=True)  34.3 us
    ppermute x3, starting transfers between devices, step(): return lax.ppermute(array, axis, [(i, (i + by) % n) for i in range(n)])  15.6 us
    all_to_all x2, starting transfers between devices, spread(): return lax.all_to_all(array, axes, split_axis=0, concat_axis=0, tiled=True)  14.1 us
    all_to_all x2, waiting for transfers between devices, spread(): return lax.all_to_all(array, axes, split_axis=0, concat_axis=0, tiled=True)  12 us
    ppermute x3, starting transfers between devices, swapped(): return lax.ppermute(array, 'c', [(0, 1), (1, 0)])  7.79 us
    pallas_call x1, Pallas kernels, gate_part(): pl.pallas_call(functools.partial(gate_kernel, orders), out_shape=(jax.Sha...  6.45 us
    ppermute x3, waiting for transfers between devices, swapped(): return lax.ppermute(array, 'c', [(0, 1), (1, 0)])  2.91 us
    reduce_sum x2, other arithmetic, summed_pieces(): return jnp.sum(pieces.astype(F32), axis=0).astype(BF16)  2.68 us
  transfers between devices with their start and end apart: 8, of which 5 were waited for; matrix products, arithmetic and copies ran while one was open for 3% of the time, Pallas kernels for 2%

profile of v2, /device:TPU:1, one launch (start us, length us, event | category | flops | bytes accessed | tf_op | source)
XLA Modules:
  0.0 105.6 jit_solution(16222452105934570256)
XLA Ops:
  0.6 1.8 %shard_map.50 = bf16[360,256]{1,0:T(8,128)(2,1)} custom-call(f32[360,256]{1,0:T(8,128)} %w_ref.1), custom_call_target="tpu_custom_call" | custom-call | tf_op jit(solution)/shard_map/pallas_call | solution.py:35
  2.4 34.3 %all_gather.3.wa_ref = bf16[1440,256]{1,0:T(8,128)(2,1)S(1)} all-gather(bf16[360,256]{1,0:T(8,128)(2,1)} %shard_map.50), channel_id=1, replica_groups=mesh['yh'=4,'yl'=2,'zl'=3,'x'=4,'zh'=4,'c'=2] {'zh'}, dimensions={0}, use_global_device_ids=true | all-gather | bytes 921600 | tf_op jit(solution)/shard_map/all_gather | solution.py:242
  36.8 3.3 %collective-permute-start = (bf16[1440,256]{1,0:T(8,128)(2,1)S(1)}, bf16[1440,256]{1,0:T(8,128)(2,1)S(1)}, u32[]{:S(2)}, u32[]{:S(2)}) collective-permute-start(bf16[1440,256]{1,0:T(8,128)(2,1)S(1)} %all_gather.3.wa_ref), channel_id=1, source_target_pairs={{0,1},{1,0},{2,3},{3,2},{4,5},{5,4},{6,7},{7,6},{8,9},{9,8},{10,11... | collective-permute-start | bytes 2211848 | tf_op jit(solution)/shard_map/ppermute | solution.py:220
  40.1 0.6 pad_add_fusion.pos_ref
  40.7 1.2 %collective-permute-done.wb_ref = bf16[1440,256]{1,0:T(8,128)(2,1)S(1)} collective-permute-done((bf16[1440,256]{1,0:T(8,128)(2,1)S(1)}, bf16[1440,256]{1,0:T(8,128)(2,1)S(1)}, u32[]{:S(2)}, u32[]{:S(2)}) %collective-permute-start) | collective-permute-done | bytes 737312 | tf_op jit(solution)/shard_map/ppermute | solution.py:220
  41.9 0.0 copy-done.3
  41.9 0.9 copy-done.4
  42.8 6.4 %shard_map.51 = (bf16[192,5120]{1,0:T(8,128)(2,1)}, bf16[72,192]{1,0:T(8,128)(2,1)}, bf16[72,192]{1,0:T(8,128)(2,1)}) custom-call(s32[2]{0:T(128)} %pad_add_fusion.pos_ref, bf16[1440,256]{1,0:T(8,128)(2,1)} %copy-done.3, bf16[1440,256]{1,0:T(8,128)(2,1)} %copy-done.4, bf16[192,5120]{1,0:T(8,128)(2,1)} %bitcast.8, bf16[72,192]{1,0:T(8,128)(2,1)} %bitcast.12), custom_call_target="tpu_custom_call" | custom-call | tf_op jit(solution)/shard_map/pallas_call | solution.py:140
  49.2 0.0 copy-start
  49.2 0.0 copy-start.5
  49.2 0.0 copy-start.1
  49.2 0.0 copy-start.2
  49.3 5.0 %all-to-all-start = ((bf16[8,24,5120]{2,1,0:T(8,128)(2,1)}), bf16[8,24,5120]{2,1,0:T(8,128)(2,1)}, u32[]{:S(2)}, u32[]{:S(2)}) async-start(bf16[8,24,5120]{2,1,0:T(8,128)(2,1)} %bitcast.11), calls=%async_computation | async-start | bytes 3932160 | tf_op jit(solution)/shard_map/all_to_all | solution.py:228
  54.3 0.0 copy-done
  54.3 2.6 %collective-permute-start.2 = (bf16[192,5120]{1,0:T(8,128)(2,1)S(1)}, bf16[192,5120]{1,0:T(8,128)(2,1)S(1)}, u32[]{:S(2)}, u32[]{:S(2)}) collective-permute-start(bf16[192,5120]{1,0:T(8,128)(2,1)S(1)} %bitcast.9), channel_id=1, source_target_pairs={{0,1},{1,0},{2,3},{3,2},{4,5},{5,4},{6,7},{7,6},{8,9},{9,8},{10,11... | collective-permute-start | bytes 5898248 | tf_op jit(solution)/shard_map/ppermute | solution.py:220
  56.9 1.9 %collective-permute-start.1 = (bf16[72,192]{1,0:T(8,128)(2,1)S(1)}, bf16[72,192]{1,0:T(8,128)(2,1)S(1)}, u32[]{:S(2)}, u32[]{:S(2)}) collective-permute-start(bf16[72,192]{1,0:T(8,128)(2,1)S(1)} %copy-done.5), channel_id=1, source_target_pairs={{0,1},{1,0},{2,3},{3,2},{4,5},{5,4},{6,7},{7,6},{8,9},{9,8},{10,11... | collective-permute-start | bytes 82952 | tf_op jit(solution)/shard_map/ppermute | solution.py:220
  58.8 1.7 %collective-permute-done.1.got_ref = bf16[72,192]{1,0:T(8,128)(2,1)S(1)} collective-permute-done((bf16[72,192]{1,0:T(8,128)(2,1)S(1)}, bf16[72,192]{1,0:T(8,128)(2,1)S(1)}, u32[]{:S(2)}, u32[]{:S(2)}) %collective-permute-start.1) | collective-permute-done | bytes 27680 | tf_op jit(solution)/shard_map/ppermute | solution.py:220
  60.5 0.0 collective-permute-done.2.xo_ref
  60.5 1.8 %shard_map.52 = (f32[360,256]{1,0:T(8,128)S(1)}, bf16[360,256]{1,0:T(8,128)(2,1)S(1)}, bf16[360,256]{1,0:T(8,128)(2,1)S(1)}, bf16[360,256]{1,0:T(8,128)(2,1)S(1)}) custom-call(s32[2]{0:T(128)S(1)} %copy-done.2, bf16[72,192]{1,0:T(8,128)(2,1)S(1)} %copy-done.1, bf16[72,192]{1,0:T(8,128)(2,1)S(1)} %collective-permute-done.1.got_ref, ...), custom_call_target="tpu_custom_call" | custom-call | tf_op jit(solution)/shard_map/pallas_call | solution.py:184
  62.3 7.3 %collective-permute-start.3 = (bf16[360,256]{1,0:T(8,128)(2,1)S(1)}, bf16[360,256]{1,0:T(8,128)(2,1)S(1)}, u32[]{:S(2)}, u32[]{:S(2)}) collective-permute-start(bf16[360,256]{1,0:T(8,128)(2,1)S(1)} %get-tuple-element.17), channel_id=1, source_target_pairs={{0,4},{2,6},{4,0},{6,2},{1,5},{3,7},{5,1},{7,3},{8,12},{10,14},{12... | collective-permute-start | bytes 552968 | tf_op jit(solution)/shard_map/ppermute | solution.py:216
  69.6 4.7 %collective-permute-start.4 = (bf16[360,256]{1,0:T(8,128)(2,1)S(1)}, bf16[360,256]{1,0:T(8,128)(2,1)S(1)}, u32[]{:S(2)}, u32[]{:S(2)}) collective-permute-start(bf16[360,256]{1,0:T(8,128)(2,1)S(1)} %get-tuple-element.18), channel_id=1, source_target_pairs={{0,2},{2,4},{4,6},{6,0},{1,3},{3,5},{5,7},{7,1},{8,10},{10,12},{12... | collective-permute-start | bytes 552968 | tf_op jit(solution)/shard_map/ppermute | solution.py:216
  74.4 3.6 %collective-permute-start.5 = (bf16[360,256]{1,0:T(8,128)(2,1)S(1)}, bf16[360,256]{1,0:T(8,128)(2,1)S(1)}, u32[]{:S(2)}, u32[]{:S(2)}) collective-permute-start(bf16[360,256]{1,0:T(8,128)(2,1)S(1)} %get-tuple-element.19), channel_id=1, source_target_pairs={{0,6},{2,0},{4,2},{6,4},{1,7},{3,1},{5,3},{7,5},{8,14},{10,8},{12,... | collective-permute-start | bytes 552968 | tf_op jit(solution)/shard_map/ppermute | solution.py:216
  77.9 1.5 %all-to-all-done = bf16[8,24,5120]{2,1,0:T(8,128)(2,1)} async-done(((bf16[8,24,5120]{2,1,0:T(8,128)(2,1)}), bf16[8,24,5120]{2,1,0:T(8,128)(2,1)}, u32[]{:S(2)}, u32[]{:S(2)}) %all-to-all-start) | async-done | bytes 1966112 | tf_op jit(solution)/shard_map/all_to_all | solution.py:228
  79.4 1.9 %reduce_sum.24 = bf16[24,5120]{1,0:T(8,128)(2,1)S(1)} reduce(bf16[8,24,5120]{2,1,0:T(8,128)(2,1)} %all-to-all-done, bf16[]{:T(256)} %constant.11.clone.1), dimensions={0}, to_apply=%region_0.0 | reduce | flops 860160 | bytes 2211842 | tf_op jit(solution)/shard_map/reduce_sum | solution.py:224
  81.3 0.8 reshape.22
  82.1 9.0 %all-to-all-start.1 = ((bf16[12,2,5120]{2,1,0:T(2,128)(2,1)}), bf16[12,2,5120]{2,1,0:T(2,128)(2,1)S(1)}, u32[]{:S(2)}, u32[]{:S(2)}) async-start(bf16[12,2,5120]{2,1,0:T(2,128)(2,1)} %reshape.22), calls=%async_computation.1 | async-start | bytes 491520 | tf_op jit(solution)/shard_map/all_to_all | solution.py:228
  91.1 0.0 collective-permute-done.3.refs_0_
  91.1 0.0 collective-permute-done.4.refs_1_
  91.1 2.3 %collective-permute-done.5.refs_2_ = bf16[360,256]{1,0:T(8,128)(2,1)S(1)} collective-permute-done((bf16[360,256]{1,0:T(8,128)(2,1)S(1)}, bf16[360,256]{1,0:T(8,128)(2,1)S(1)}, u32[]{:S(2)}, u32[]{:S(2)}) %collective-permute-start.5) | collective-permute-done | bytes 184352 | tf_op jit(solution)/shard_map/ppermute | solution.py:216
  93.5 0.8 shard_map.53
  94.3 10.5 %all-to-all-done.1 = bf16[12,2,5120]{2,1,0:T(2,128)(2,1)S(1)} async-done(((bf16[12,2,5120]{2,1,0:T(2,128)(2,1)}), bf16[12,2,5120]{2,1,0:T(2,128)(2,1)S(1)}, u32[]{:S(2)}, u32[]{:S(2)}) %all-to-all-start.1) | async-done | bytes 245792 | tf_op jit(solution)/shard_map/all_to_all | solution.py:228
  104.8 0.8 reduce_sum.25
  (5 shorter events, 0.0 us)
Async XLA Ops:
  36.8 5.1 %copy-start.3 = (bf16[1440,256]{1,0:T(8,128)(2,1)}, bf16[1440,256]{1,0:T(8,128)(2,1)S(1)}, u32[]{:S(2)}) copy-start(bf16[1440,256]{1,0:T(8,128)(2,1)S(1)} %all_gather.3.wa_ref) | copy-start | bytes 2211844
  36.8 5.1 %collective-permute-start = (bf16[1440,256]{1,0:T(8,128)(2,1)S(1)}, bf16[1440,256]{1,0:T(8,128)(2,1)S(1)}, u32[]{:S(2)}, u32[]{:S(2)}) collective-permute-start(bf16[1440,256]{1,0:T(8,128)(2,1)S(1)} %all_gather.3.wa_ref), channel_id=1, source_target_pairs={{0,1},{1,0},{2,3},{3,2},{4,5},{5,4},{6,7},{7,6},{8,9},{9,8},{10,11... | collective-permute-start | bytes 2211848 | tf_op jit(solution)/shard_map/ppermute | solution.py:220
  41.9 0.9 copy-start.4
  49.2 5.1 %copy-start = (bf16[1,192,1,5120]{3,1,2,0:T(8,128)(2,1)S(1)}, bf16[1,192,1,5120]{3,1,2,0:T(8,128)(2,1)}, u32[]{:S(2)}) copy-start(bf16[1,192,1,5120]{3,1,2,0:T(8,128)(2,1)} %param.3) | copy-start | bytes 5898244
  49.2 7.6 %copy-start.5 = (bf16[72,192]{1,0:T(8,128)(2,1)S(1)}, bf16[72,192]{1,0:T(8,128)(2,1)}, u32[]{:S(2)}) copy-start(bf16[72,192]{1,0:T(8,128)(2,1)} %get-tuple-element.14) | copy-start | bytes 82948
  49.2 11.3 %copy-start.1 = (bf16[72,192]{1,0:T(8,128)(2,1)S(1)}, bf16[72,192]{1,0:T(8,128)(2,1)}, u32[]{:S(2)}) copy-start(bf16[72,192]{1,0:T(8,128)(2,1)} %get-tuple-element.13.mine_ref) | copy-start | bytes 82948
  49.2 11.3 %copy-start.2 = (s32[2]{0:T(128)S(1)}, s32[2]{0:T(128)}, u32[]{:S(2)}) copy-start(s32[2]{0:T(128)} %pad_add_fusion.pos_ref) | copy-start | bytes 28
  49.3 30.2 %all-to-all-start = ((bf16[8,24,5120]{2,1,0:T(8,128)(2,1)}), bf16[8,24,5120]{2,1,0:T(8,128)(2,1)}, u32[]{:S(2)}, u32[]{:S(2)}) async-start(bf16[8,24,5120]{2,1,0:T(8,128)(2,1)} %bitcast.11), calls=%async_computation | async-start | bytes 3932160 | tf_op jit(solution)/shard_map/all_to_all | solution.py:228
  54.3 6.2 %collective-permute-start.2 = (bf16[192,5120]{1,0:T(8,128)(2,1)S(1)}, bf16[192,5120]{1,0:T(8,128)(2,1)S(1)}, u32[]{:S(2)}, u32[]{:S(2)}) collective-permute-start(bf16[192,5120]{1,0:T(8,128)(2,1)S(1)} %bitcast.9), channel_id=1, source_target_pairs={{0,1},{1,0},{2,3},{3,2},{4,5},{5,4},{6,7},{7,6},{8,9},{9,8},{10,11... | collective-permute-start | bytes 5898248 | tf_op jit(solution)/shard_map/ppermute | solution.py:220
  56.9 3.6 %collective-permute-start.1 = (bf16[72,192]{1,0:T(8,128)(2,1)S(1)}, bf16[72,192]{1,0:T(8,128)(2,1)S(1)}, u32[]{:S(2)}, u32[]{:S(2)}) collective-permute-start(bf16[72,192]{1,0:T(8,128)(2,1)S(1)} %copy-done.5), channel_id=1, source_target_pairs={{0,1},{1,0},{2,3},{3,2},{4,5},{5,4},{6,7},{7,6},{8,9},{9,8},{10,11... | collective-permute-start | bytes 82952 | tf_op jit(solution)/shard_map/ppermute | solution.py:220
  62.3 28.8 %collective-permute-start.3 = (bf16[360,256]{1,0:T(8,128)(2,1)S(1)}, bf16[360,256]{1,0:T(8,128)(2,1)S(1)}, u32[]{:S(2)}, u32[]{:S(2)}) collective-permute-start(bf16[360,256]{1,0:T(8,128)(2,1)S(1)} %get-tuple-element.17), channel_id=1, source_target_pairs={{0,4},{2,6},{4,0},{6,2},{1,5},{3,7},{5,1},{7,3},{8,12},{10,14},{12... | collective-permute-start | bytes 552968 | tf_op jit(solution)/shard_map/ppermute | solution.py:216
  69.6 21.5 %collective-permute-start.4 = (bf16[360,256]{1,0:T(8,128)(2,1)S(1)}, bf16[360,256]{1,0:T(8,128)(2,1)S(1)}, u32[]{:S(2)}, u32[]{:S(2)}) collective-permute-start(bf16[360,256]{1,0:T(8,128)(2,1)S(1)} %get-tuple-element.18), channel_id=1, source_target_pairs={{0,2},{2,4},{4,6},{6,0},{1,3},{3,5},{5,7},{7,1},{8,10},{10,12},{12... | collective-permute-start | bytes 552968 | tf_op jit(solution)/shard_map/ppermute | solution.py:216
  74.4 19.1 %collective-permute-start.5 = (bf16[360,256]{1,0:T(8,128)(2,1)S(1)}, bf16[360,256]{1,0:T(8,128)(2,1)S(1)}, u32[]{:S(2)}, u32[]{:S(2)}) collective-permute-start(bf16[360,256]{1,0:T(8,128)(2,1)S(1)} %get-tuple-element.19), channel_id=1, source_target_pairs={{0,6},{2,0},{4,2},{6,4},{1,7},{3,1},{5,3},{7,5},{8,14},{10,8},{12,... | collective-permute-start | bytes 552968 | tf_op jit(solution)/shard_map/ppermute | solution.py:216
  82.1 22.7 %all-to-all-start.1 = ((bf16[12,2,5120]{2,1,0:T(2,128)(2,1)}), bf16[12,2,5120]{2,1,0:T(2,128)(2,1)S(1)}, u32[]{:S(2)}, u32[]{:S(2)}) async-start(bf16[12,2,5120]{2,1,0:T(2,128)(2,1)} %reshape.22), calls=%async_computation.1 | async-start | bytes 491520 | tf_op jit(solution)/shard_map/all_to_all | solution.py:228

commit v3 on v2

--- a/solution.py
+++ b/solution.py
@@ -16,9 +16,7 @@
 F32 = jnp.float32
 BF16 = jnp.bfloat16
 VMEM = pl.BlockSpec(memory_space=pltpu.VMEM)
-HBM = pl.BlockSpec(memory_space=pltpu.HBM)
-SPANS = 5
-PARAMS = pltpu.CompilerParams(vmem_limit_bytes=40 << 20)
+PARAMS = pltpu.CompilerParams(vmem_limit_bytes=16 << 20)
 
 
 def requantized(blocks):
@@ -37,6 +35,8 @@
         out_shape=jax.ShapeDtypeStruct(weight.shape, BF16),
         in_specs=[VMEM],
         out_specs=VMEM,
+        cost_estimate=pl.CostEstimate(flops=10**10, bytes_accessed=0, transcendentals=0),
+        compiler_params=PARAMS,
     )(weight)
 
 
@@ -61,21 +61,8 @@
     return (source == old).astype(F32).astype(BF16)
 
 
-def gate_kernel(orders, pos_ref, wa_ref, wb_ref, x_hbm, c_ref, part_hbm, keep_ref, send_ref, *scratch):
-    w32, wmat, x_ref, part_ref, sem_in, sem_out = scratch
+def gate_kernel(orders, pos_ref, wa_ref, wb_ref, x_ref, c_ref, part_ref, keep_ref, send_ref, w32, wmat):
     core = pos_ref[1]
-    span = x_ref.shape[1] // SPANS
-    spans = [slice(i * span, (i + 1) * span) for i in range(SPANS)]
-    loads = [
-        pltpu.make_async_copy(x_hbm.at[:, at], x_ref.at[:, at], sem_in.at[i])
-        for i, at in enumerate(spans)
-    ]
-    stores = [
-        pltpu.make_async_copy(part_ref.at[:, at], part_hbm.at[:, at], sem_out.at[i])
-        for i, at in enumerate(spans)
-    ]
-    for load in loads:
-        load.start()
     rows = wmat.shape[0]
     chunk, block = wa_ref.shape
     per_row = w32.shape[1] // rows
@@ -88,8 +75,6 @@
     proj = jnp.zeros((rows, x_ref.shape[0]), F32)
     for b in range(per_row):
         columns = slice(b * block, (b + 1) * block)
-        if b * block % span == 0:
-            loads[b * block // span].wait()
         w = jnp.concatenate(
             [w32[k, pl.ds(b, rows, stride=per_row), :] for k in range(halves)], axis=1
         ).astype(BF16)
@@ -127,10 +112,6 @@
         part_ref[:, columns] = jnp.dot(
             pre, wmat[:, columns], preferred_element_type=F32
         ).astype(BF16)
-        if (b + 1) * block % span == 0:
-            stores[b * block // span].start()
-    for store in stores:
-        store.wait()
 
 
 def gate_part(orders, pos, w_mine, w_other, x, cot):
@@ -144,17 +125,13 @@
             jax.ShapeDtypeStruct((rows // 2, tokens), BF16),
             jax.ShapeDtypeStruct((rows // 2, tokens), BF16),
         ),
-        in_specs=[pl.BlockSpec(memory_space=pltpu.SMEM), VMEM, VMEM, HBM, VMEM],
-        out_specs=(HBM, VMEM, VMEM),
+        in_specs=[pl.BlockSpec(memory_space=pltpu.SMEM), VMEM, VMEM, VMEM, VMEM],
+        out_specs=(VMEM, VMEM, VMEM),
         scratch_shapes=[
             pltpu.VMEM((block // LANES, 2 * w_mine.shape[0], LANES), F32),
             pltpu.VMEM((rows, width), BF16),
-            pltpu.VMEM((tokens, width), BF16),
-            pltpu.VMEM((tokens, width), BF16),
-            pltpu.SemaphoreType.DMA((SPANS,)),
-            pltpu.SemaphoreType.DMA((SPANS,)),
         ],
-        compiler_params=pltpu.CompilerParams(vmem_limit_bytes=61_600_000),
+        compiler_params=PARAMS,
     )(pos, w_mine, w_other, x, cot)
 
 

time: 106 us -> 102 us (0.962)
  Pallas kernels: 10.9 us -> 5.75 us
  local copies, waits for them, and re-layouts: 1.68 us -> 3.03 us
    pallas_call x1, Pallas kernels: 6.45 us -> 3 us  [gate_part(): pl.pallas_call(functools.partial(gate_kernel, orders), out_shape=(jax.Sha...]
    pallas_call x1, Pallas kernels: 1.82 us -> 0.15 us  [quantize_weight(): pl.pallas_call(quantize_kernel, out_shape=jax.ShapeDtypeStruct(weight.sha...]
    unnamed x12 -> x8, local copies, waits for them, and re-layouts: 0.88 us -> 2.24 us
  transfers between devices with their start and end apart: 8 -> 8, of which waited for: 5 -> 5; matrix products, arithmetic and copies ran while one was open for 3% -> 3% of each run, Pallas kernels for 2% -> 3%
where the time goes in v3:
time: 102 us
  starting transfers between devices  37.3 us (37%)
  blocking collectives  34.2 us (34%)
  waiting for transfers between devices  17.8 us (17%)
  Pallas kernels  5.75 us (6%)
  local copies, waits for them, and re-layouts  3.03 us (3%)
  other arithmetic  2.76 us (3%)
    all_gather x1, blocking collectives, body(): w_mine = lax.all_gather(own, 'zh', axis=0, tiled=True)  34.2 us
    ppermute x3, starting transfers between devices, step(): return lax.ppermute(array, axis, [(i, (i + by) % n) for i in range(n)])  15.6 us
    all_to_all x2, starting transfers between devices, spread(): return lax.all_to_all(array, axes, split_axis=0, concat_axis=0, tiled=True)  13.9 us
    all_to_all x2, waiting for transfers between devices, spread(): return lax.all_to_all(array, axes, split_axis=0, concat_axis=0, tiled=True)  11.9 us
    ppermute x3, starting transfers between devices, swapped(): return lax.ppermute(array, 'c', [(0, 1), (1, 0)])  7.78 us
    ppermute x3, waiting for transfers between devices, swapped(): return lax.ppermute(array, 'c', [(0, 1), (1, 0)])  3.44 us
    pallas_call x1, Pallas kernels, gate_part(): pl.pallas_call(functools.partial(gate_kernel, orders), out_shape=(jax.Sha...  3 us
    reduce_sum x2, other arithmetic, summed_pieces(): return jnp.sum(pieces.astype(F32), axis=0).astype(BF16)  2.68 us
  transfers between devices with their start and end apart: 8, of which 5 were waited for; matrix products, arithmetic and copies ran while one was open for 3% of the time, Pallas kernels for 3%

profile of v3, /device:TPU:1, one launch (start us, length us, event | category | flops | bytes accessed | tf_op | source)
XLA Modules:
  0.0 101.6 jit_solution(13629059386968431292)
XLA Ops:
  0.6 0.0 copy-start.3
  0.6 1.0 copy-done.3
  1.6 0.0 copy-start
  1.6 0.2 shard_map.50
  1.8 34.2 %all_gather.3.wa_ref = bf16[1440,256]{1,0:T(8,128)(2,1)S(1)} all-gather(bf16[360,256]{1,0:T(8,128)(2,1)S(1)} %shard_map.50), channel_id=1, replica_groups=mesh['yh'=4,'yl'=2,'zl'=3,'x'=4,'zh'=4,'c'=2] {'zh'}, dimensions={0}, use_global_device_ids=true | all-gather | bytes 921600 | tf_op jit(solution)/shard_map/all_gather | solution.py:219
  36.0 3.3 %collective-permute-start = (bf16[1440,256]{1,0:T(8,128)(2,1)S(1)}, bf16[1440,256]{1,0:T(8,128)(2,1)S(1)}, u32[]{:S(2)}, u32[]{:S(2)}) collective-permute-start(bf16[1440,256]{1,0:T(8,128)(2,1)S(1)} %all_gather.3.wa_ref), channel_id=1, source_target_pairs={{0,1},{1,0},{2,3},{3,2},{4,5},{5,4},{6,7},{7,6},{8,9},{9,8},{10,11... | collective-permute-start | bytes 2211848 | tf_op jit(solution)/shard_map/ppermute | solution.py:197
  39.4 0.1 pad_add_fusion.pos_ref
  39.4 1.7 %collective-permute-done.wb_ref = bf16[1440,256]{1,0:T(8,128)(2,1)S(1)} collective-permute-done((bf16[1440,256]{1,0:T(8,128)(2,1)S(1)}, bf16[1440,256]{1,0:T(8,128)(2,1)S(1)}, u32[]{:S(2)}, u32[]{:S(2)}) %collective-permute-start) | collective-permute-done | bytes 737312 | tf_op jit(solution)/shard_map/ppermute | solution.py:197
  41.2 0.0 copy-done
  41.2 0.0 copy-done.2
  41.2 3.0 %shard_map.51 = (bf16[192,5120]{1,0:T(8,128)(2,1)S(1)}, bf16[72,192]{1,0:T(8,128)(2,1)S(1)}, bf16[72,192]{1,0:T(8,128)(2,1)S(1)}) custom-call(s32[2]{0:T(128)S(1)} %pad_add_fusion.pos_ref, bf16[1440,256]{1,0:T(8,128)(2,1)S(1)} %all_gather.3.wa_ref, bf16[1440,256]{1,0:T(8,128)(2,1)S(1)} %collective-permute-done.wb_ref, bf16[192,5120]{1,0:T(8,128)(2,1)S(1)} %bitcast.8, ...), custom_call_target="tpu_custom_call" | custom-call | tf_op jit(solution)/shard_map/pallas_call | solution.py:121
  44.2 0.0 copy-start.1
  44.2 1.3 %copy-done.1 = bf16[192,5120]{1,0:T(8,128)(2,1)} copy-done((bf16[192,5120]{1,0:T(8,128)(2,1)}, bf16[192,5120]{1,0:T(8,128)(2,1)S(1)}, u32[]{:S(2)}) %copy-start.1) | copy-done | bytes 1966104
  45.4 4.9 %all-to-all-start = ((bf16[8,24,5120]{2,1,0:T(8,128)(2,1)}), bf16[8,24,5120]{2,1,0:T(8,128)(2,1)}, u32[]{:S(2)}, u32[]{:S(2)}) async-start(bf16[8,24,5120]{2,1,0:T(8,128)(2,1)} %bitcast.11), calls=%async_computation | async-start | bytes 3932160 | tf_op jit(solution)/shard_map/all_to_all | solution.py:205
  50.3 2.5 %collective-permute-start.2 = (bf16[192,5120]{1,0:T(8,128)(2,1)S(1)}, bf16[192,5120]{1,0:T(8,128)(2,1)S(1)}, u32[]{:S(2)}, u32[]{:S(2)}) collective-permute-start(bf16[192,5120]{1,0:T(8,128)(2,1)S(1)} %bitcast.9), channel_id=1, source_target_pairs={{0,1},{1,0},{2,3},{3,2},{4,5},{5,4},{6,7},{7,6},{8,9},{9,8},{10,11... | collective-permute-start | bytes 5898248 | tf_op jit(solution)/shard_map/ppermute | solution.py:197
  52.9 1.9 %collective-permute-start.1 = (bf16[72,192]{1,0:T(8,128)(2,1)S(1)}, bf16[72,192]{1,0:T(8,128)(2,1)S(1)}, u32[]{:S(2)}, u32[]{:S(2)}) collective-permute-start(bf16[72,192]{1,0:T(8,128)(2,1)S(1)} %get-tuple-element.14), channel_id=1, source_target_pairs={{0,1},{1,0},{2,3},{3,2},{4,5},{5,4},{6,7},{7,6},{8,9},{9,8},{10,11... | collective-permute-start | bytes 82952 | tf_op jit(solution)/shard_map/ppermute | solution.py:197
  54.8 1.7 %collective-permute-done.1.got_ref = bf16[72,192]{1,0:T(8,128)(2,1)S(1)} collective-permute-done((bf16[72,192]{1,0:T(8,128)(2,1)S(1)}, bf16[72,192]{1,0:T(8,128)(2,1)S(1)}, u32[]{:S(2)}, u32[]{:S(2)}) %collective-permute-start.1) | collective-permute-done | bytes 27680 | tf_op jit(solution)/shard_map/ppermute | solution.py:197
  56.5 0.0 collective-permute-done.2.xo_ref
  56.5 1.8 %shard_map.52 = (f32[360,256]{1,0:T(8,128)S(1)}, bf16[360,256]{1,0:T(8,128)(2,1)S(1)}, bf16[360,256]{1,0:T(8,128)(2,1)S(1)}, bf16[360,256]{1,0:T(8,128)(2,1)S(1)}) custom-call(s32[2]{0:T(128)S(1)} %pad_add_fusion.pos_ref, bf16[72,192]{1,0:T(8,128)(2,1)S(1)} %get-tuple-element.13.mine_ref, bf16[72,192]{1,0:T(8,128)(2,1)S(1)} %collective-permute-done.1.got_ref, ...), custom_call_target="tpu_custom_call" | custom-call | tf_op jit(solution)/shard_map/pallas_call | solution.py:161
  58.3 7.3 %collective-permute-start.3 = (bf16[360,256]{1,0:T(8,128)(2,1)S(1)}, bf16[360,256]{1,0:T(8,128)(2,1)S(1)}, u32[]{:S(2)}, u32[]{:S(2)}) collective-permute-start(bf16[360,256]{1,0:T(8,128)(2,1)S(1)} %get-tuple-element.17), channel_id=1, source_target_pairs={{0,4},{2,6},{4,0},{6,2},{1,5},{3,7},{5,1},{7,3},{8,12},{10,14},{12... | collective-permute-start | bytes 552968 | tf_op jit(solution)/shard_map/ppermute | solution.py:193
  65.6 4.7 %collective-permute-start.4 = (bf16[360,256]{1,0:T(8,128)(2,1)S(1)}, bf16[360,256]{1,0:T(8,128)(2,1)S(1)}, u32[]{:S(2)}, u32[]{:S(2)}) collective-permute-start(bf16[360,256]{1,0:T(8,128)(2,1)S(1)} %get-tuple-element.18), channel_id=1, source_target_pairs={{0,2},{2,4},{4,6},{6,0},{1,3},{3,5},{5,7},{7,1},{8,10},{10,12},{12... | collective-permute-start | bytes 552968 | tf_op jit(solution)/shard_map/ppermute | solution.py:193
  70.3 3.6 %collective-permute-start.5 = (bf16[360,256]{1,0:T(8,128)(2,1)S(1)}, bf16[360,256]{1,0:T(8,128)(2,1)S(1)}, u32[]{:S(2)}, u32[]{:S(2)}) collective-permute-start(bf16[360,256]{1,0:T(8,128)(2,1)S(1)} %get-tuple-element.19), channel_id=1, source_target_pairs={{0,6},{2,0},{4,2},{6,4},{1,7},{3,1},{5,3},{7,5},{8,14},{10,8},{12,... | collective-permute-start | bytes 552968 | tf_op jit(solution)/shard_map/ppermute | solution.py:193
  73.9 1.5 %all-to-all-done = bf16[8,24,5120]{2,1,0:T(8,128)(2,1)} async-done(((bf16[8,24,5120]{2,1,0:T(8,128)(2,1)}), bf16[8,24,5120]{2,1,0:T(8,128)(2,1)}, u32[]{:S(2)}, u32[]{:S(2)}) %all-to-all-start) | async-done | bytes 1966112 | tf_op jit(solution)/shard_map/all_to_all | solution.py:205
  75.5 1.9 %reduce_sum.24 = bf16[24,5120]{1,0:T(8,128)(2,1)S(1)} reduce(bf16[8,24,5120]{2,1,0:T(8,128)(2,1)} %all-to-all-done, bf16[]{:T(256)} %constant.11.clone.1), dimensions={0}, to_apply=%region_0.0 | reduce | flops 860160 | bytes 2211842 | tf_op jit(solution)/shard_map/reduce_sum | solution.py:201
  77.3 0.8 reshape.22
  78.1 9.0 %all-to-all-start.1 = ((bf16[12,2,5120]{2,1,0:T(2,128)(2,1)}), bf16[12,2,5120]{2,1,0:T(2,128)(2,1)S(1)}, u32[]{:S(2)}, u32[]{:S(2)}) async-start(bf16[12,2,5120]{2,1,0:T(2,128)(2,1)} %reshape.22), calls=%async_computation.1 | async-start | bytes 491520 | tf_op jit(solution)/shard_map/all_to_all | solution.py:205
  87.1 0.0 collective-permute-done.3.refs_0_
  87.1 0.0 collective-permute-done.4.refs_1_
  87.1 2.4 %collective-permute-done.5.refs_2_ = bf16[360,256]{1,0:T(8,128)(2,1)S(1)} collective-permute-done((bf16[360,256]{1,0:T(8,128)(2,1)S(1)}, bf16[360,256]{1,0:T(8,128)(2,1)S(1)}, u32[]{:S(2)}, u32[]{:S(2)}) %collective-permute-start.5) | collective-permute-done | bytes 184352 | tf_op jit(solution)/shard_map/ppermute | solution.py:193
  89.5 0.8 shard_map.53
  90.4 10.4 %all-to-all-done.1 = bf16[12,2,5120]{2,1,0:T(2,128)(2,1)S(1)} async-done(((bf16[12,2,5120]{2,1,0:T(2,128)(2,1)}), bf16[12,2,5120]{2,1,0:T(2,128)(2,1)S(1)}, u32[]{:S(2)}, u32[]{:S(2)}) %all-to-all-start.1) | async-done | bytes 245792 | tf_op jit(solution)/shard_map/all_to_all | solution.py:205
  100.8 0.8 reduce_sum.25
  (1 shorter events, 0.0 us)
Async XLA Ops:
  0.6 1.0 copy-start.3
  1.6 39.6 %copy-start = (bf16[1,192,1,5120]{3,1,2,0:T(8,128)(2,1)S(1)}, bf16[1,192,1,5120]{3,1,2,0:T(8,128)(2,1)}, u32[]{:S(2)}) copy-start(bf16[1,192,1,5120]{3,1,2,0:T(8,128)(2,1)} %param.3) | copy-start | bytes 5898244
  1.6 39.6 %copy-start.2 = (bf16[1,192,1,72]{1,3,2,0:T(8,128)(2,1)S(1)}, bf16[1,192,1,72]{1,3,2,0:T(8,128)(2,1)}, u32[]{:S(2)}) copy-start(bf16[1,192,1,72]{1,3,2,0:T(8,128)(2,1)} %param.4) | copy-start | bytes 82948
  36.0 5.1 %collective-permute-start = (bf16[1440,256]{1,0:T(8,128)(2,1)S(1)}, bf16[1440,256]{1,0:T(8,128)(2,1)S(1)}, u32[]{:S(2)}, u32[]{:S(2)}) collective-permute-start(bf16[1440,256]{1,0:T(8,128)(2,1)S(1)} %all_gather.3.wa_ref), channel_id=1, source_target_pairs={{0,1},{1,0},{2,3},{3,2},{4,5},{5,4},{6,7},{7,6},{8,9},{9,8},{10,11... | collective-permute-start | bytes 2211848 | tf_op jit(solution)/shard_map/ppermute | solution.py:197
  44.2 1.3 %copy-start.1 = (bf16[192,5120]{1,0:T(8,128)(2,1)}, bf16[192,5120]{1,0:T(8,128)(2,1)S(1)}, u32[]{:S(2)}) copy-start(bf16[192,5120]{1,0:T(8,128)(2,1)S(1)} %get-tuple-element.20) | copy-start | bytes 5898244
  45.4 30.0 %all-to-all-start = ((bf16[8,24,5120]{2,1,0:T(8,128)(2,1)}), bf16[8,24,5120]{2,1,0:T(8,128)(2,1)}, u32[]{:S(2)}, u32[]{:S(2)}) async-start(bf16[8,24,5120]{2,1,0:T(8,128)(2,1)} %bitcast.11), calls=%async_computation | async-start | bytes 3932160 | tf_op jit(solution)/shard_map/all_to_all | solution.py:205
  50.3 6.2 %collective-permute-start.2 = (bf16[192,5120]{1,0:T(8,128)(2,1)S(1)}, bf16[192,5120]{1,0:T(8,128)(2,1)S(1)}, u32[]{:S(2)}, u32[]{:S(2)}) collective-permute-start(bf16[192,5120]{1,0:T(8,128)(2,1)S(1)} %bitcast.9), channel_id=1, source_target_pairs={{0,1},{1,0},{2,3},{3,2},{4,5},{5,4},{6,7},{7,6},{8,9},{9,8},{10,11... | collective-permute-start | bytes 5898248 | tf_op jit(solution)/shard_map/ppermute | solution.py:197
  52.9 3.6 %collective-permute-start.1 = (bf16[72,192]{1,0:T(8,128)(2,1)S(1)}, bf16[72,192]{1,0:T(8,128)(2,1)S(1)}, u32[]{:S(2)}, u32[]{:S(2)}) collective-permute-start(bf16[72,192]{1,0:T(8,128)(2,1)S(1)} %get-tuple-element.14), channel_id=1, source_target_pairs={{0,1},{1,0},{2,3},{3,2},{4,5},{5,4},{6,7},{7,6},{8,9},{9,8},{10,11... | collective-permute-start | bytes 82952 | tf_op jit(solution)/shard_map/ppermute | solution.py:197
  58.3 28.8 %collective-permute-start.3 = (bf16[360,256]{1,0:T(8,128)(2,1)S(1)}, bf16[360,256]{1,0:T(8,128)(2,1)S(1)}, u32[]{:S(2)}, u32[]{:S(2)}) collective-permute-start(bf16[360,256]{1,0:T(8,128)(2,1)S(1)} %get-tuple-element.17), channel_id=1, source_target_pairs={{0,4},{2,6},{4,0},{6,2},{1,5},{3,7},{5,1},{7,3},{8,12},{10,14},{12... | collective-permute-start | bytes 552968 | tf_op jit(solution)/shard_map/ppermute | solution.py:193
  65.6 21.5 %collective-permute-start.4 = (bf16[360,256]{1,0:T(8,128)(2,1)S(1)}, bf16[360,256]{1,0:T(8,128)(2,1)S(1)}, u32[]{:S(2)}, u32[]{:S(2)}) collective-permute-start(bf16[360,256]{1,0:T(8,128)(2,1)S(1)} %get-tuple-element.18), channel_id=1, source_target_pairs={{0,2},{2,4},{4,6},{6,0},{1,3},{3,5},{5,7},{7,1},{8,10},{10,12},{12... | collective-permute-start | bytes 552968 | tf_op jit(solution)/shard_map/ppermute | solution.py:193
  70.3 19.2 %collective-permute-start.5 = (bf16[360,256]{1,0:T(8,128)(2,1)S(1)}, bf16[360,256]{1,0:T(8,128)(2,1)S(1)}, u32[]{:S(2)}, u32[]{:S(2)}) collective-permute-start(bf16[360,256]{1,0:T(8,128)(2,1)S(1)} %get-tuple-element.19), channel_id=1, source_target_pairs={{0,6},{2,0},{4,2},{6,4},{1,7},{3,1},{5,3},{7,5},{8,14},{10,8},{12,... | collective-permute-start | bytes 552968 | tf_op jit(solution)/shard_map/ppermute | solution.py:193
  78.1 22.7 %all-to-all-start.1 = ((bf16[12,2,5120]{2,1,0:T(2,128)(2,1)}), bf16[12,2,5120]{2,1,0:T(2,128)(2,1)S(1)}, u32[]{:S(2)}, u32[]{:S(2)}) async-start(bf16[12,2,5120]{2,1,0:T(2,128)(2,1)} %reshape.22), calls=%async_computation.1 | async-start | bytes 491520 | tf_op jit(solution)/shard_map/all_to_all | solution.py:205

commit v4 on v3

--- a/solution.py
+++ b/solution.py
@@ -16,6 +16,7 @@
 F32 = jnp.float32
 BF16 = jnp.bfloat16
 VMEM = pl.BlockSpec(memory_space=pltpu.VMEM)
+SPANS = 10
 PARAMS = pltpu.CompilerParams(vmem_limit_bytes=16 << 20)
 
 
@@ -61,9 +62,14 @@
     return (source == old).astype(F32).astype(BF16)
 
 
-def gate_kernel(orders, pos_ref, wa_ref, wb_ref, x_ref, c_ref, part_ref, keep_ref, send_ref, w32, wmat):
+def gate_kernel(orders, pos_ref, wa_ref, wb_ref, x_ref, c_ref, part_hbm, keep_ref, send_ref, w32, wmat, part_ref, sem):
     core = pos_ref[1]
     rows = wmat.shape[0]
+    span = part_ref.shape[1] // SPANS
+    stores = []
+    for i in range(SPANS):
+        at = slice(i * span, (i + 1) * span)
+        stores.append(pltpu.make_async_copy(part_ref.at[:, at], part_hbm.at[:, at], sem.at[i]))
     chunk, block = wa_ref.shape
     per_row = w32.shape[1] // rows
     lanes = w32.shape[2]
@@ -112,6 +118,10 @@
         part_ref[:, columns] = jnp.dot(
             pre, wmat[:, columns], preferred_element_type=F32
         ).astype(BF16)
+        if (b + 1) * block % span == 0:
+            stores[b * block // span].start()
+    for store in stores:
+        store.wait()
 
 
 def gate_part(orders, pos, w_mine, w_other, x, cot):
@@ -121,17 +131,19 @@
     return pl.pallas_call(
         functools.partial(gate_kernel, orders),
         out_shape=(
-            jax.ShapeDtypeStruct((tokens, width), BF16),
+            pltpu.HBM((tokens, width), BF16),
             jax.ShapeDtypeStruct((rows // 2, tokens), BF16),
             jax.ShapeDtypeStruct((rows // 2, tokens), BF16),
         ),
         in_specs=[pl.BlockSpec(memory_space=pltpu.SMEM), VMEM, VMEM, VMEM, VMEM],
-        out_specs=(VMEM, VMEM, VMEM),
+        out_specs=(pl.BlockSpec(memory_space=pltpu.HBM), VMEM, VMEM),
         scratch_shapes=[
             pltpu.VMEM((block // LANES, 2 * w_mine.shape[0], LANES), F32),
             pltpu.VMEM((rows, width), BF16),
+            pltpu.VMEM((tokens, width), BF16),
+            pltpu.SemaphoreType.DMA((SPANS,)),
         ],
-        compiler_params=PARAMS,
+        compiler_params=pltpu.CompilerParams(vmem_limit_bytes=16 << 20),
     )(pos, w_mine, w_other, x, cot)
 
 

time: 102 us -> 102 us (level)
  local copies, waits for them, and re-layouts: 3.03 us -> 1.77 us
    unnamed x8 -> x6, local copies, waits for them, and re-layouts: 2.24 us -> 0.99 us
where the time goes in v4:
time: 102 us; the launch traced here: 101 us
  starting transfers between devices  37.2 us (36%)
  blocking collectives  34.2 us (34%)
  waiting for transfers between devices  17.8 us (17%)
  Pallas kernels  6.59 us (6%)
  other arithmetic  2.76 us (3%)
  local copies, waits for them, and re-layouts  1.77 us (2%)
    all_gather x1, blocking collectives, body(): w_mine = lax.all_gather(own, 'zh', axis=0, tiled=True)  34.2 us
    ppermute x3, starting transfers between devices, step(): return lax.ppermute(array, axis, [(i, (i + by) % n) for i in range(n)])  15.6 us
    all_to_all x2, starting transfers between devices, spread(): return lax.all_to_all(array, axes, split_axis=0, concat_axis=0, tiled=True)  13.9 us
    all_to_all x2, waiting for transfers between devices, spread(): return lax.all_to_all(array, axes, split_axis=0, concat_axis=0, tiled=True)  12 us
    ppermute x3, starting transfers between devices, swapped(): return lax.ppermute(array, 'c', [(0, 1), (1, 0)])  7.78 us
    pallas_call x1, Pallas kernels, gate_part(): pl.pallas_call(functools.partial(gate_kernel, orders), out_shape=(pltpu.H...  3.81 us
    ppermute x3, waiting for transfers between devices, swapped(): return lax.ppermute(array, 'c', [(0, 1), (1, 0)])  3.44 us
    reduce_sum x2, other arithmetic, summed_pieces(): return jnp.sum(pieces.astype(F32), axis=0).astype(BF16)  2.68 us
  transfers between devices with their start and end apart: 8, of which 5 were waited for; matrix products, arithmetic and copies ran while one was open for 3% of the time, Pallas kernels for 3%

profile of v4, /device:TPU:1, one launch (start us, length us, event | category | flops | bytes accessed | tf_op | source)
XLA Modules:
  0.0 101.2 jit_solution(316198871651159484)
XLA Ops:
  0.6 0.0 copy-start.2
  0.6 1.0 copy-done.2
  1.6 0.0 copy-start
  1.6 0.0 copy-start.1
  1.6 0.2 shard_map.50
  1.8 34.2 %all_gather.3.wa_ref = bf16[1440,256]{1,0:T(8,128)(2,1)S(1)} all-gather(bf16[360,256]{1,0:T(8,128)(2,1)S(1)} %shard_map.50), channel_id=1, replica_groups=mesh['yh'=4,'yl'=2,'zl'=3,'x'=4,'zh'=4,'c'=2] {'zh'}, dimensions={0}, use_global_device_ids=true | all-gather | bytes 921600 | tf_op jit(solution)/shard_map/all_gather | solution.py:231
  36.0 3.3 %collective-permute-start = (bf16[1440,256]{1,0:T(8,128)(2,1)S(1)}, bf16[1440,256]{1,0:T(8,128)(2,1)S(1)}, u32[]{:S(2)}, u32[]{:S(2)}) collective-permute-start(bf16[1440,256]{1,0:T(8,128)(2,1)S(1)} %all_gather.3.wa_ref), channel_id=1, source_target_pairs={{0,1},{1,0},{2,3},{3,2},{4,5},{5,4},{6,7},{7,6},{8,9},{9,8},{10,11... | collective-permute-start | bytes 2211848 | tf_op jit(solution)/shard_map/ppermute | solution.py:209
  39.4 0.1 pad_add_fusion.pos_ref
  39.4 1.7 %collective-permute-done.wb_ref = bf16[1440,256]{1,0:T(8,128)(2,1)S(1)} collective-permute-done((bf16[1440,256]{1,0:T(8,128)(2,1)S(1)}, bf16[1440,256]{1,0:T(8,128)(2,1)S(1)}, u32[]{:S(2)}, u32[]{:S(2)}) %collective-permute-start) | collective-permute-done | bytes 737312 | tf_op jit(solution)/shard_map/ppermute | solution.py:209
  41.2 0.0 copy-done
  41.2 0.0 copy-done.1
  41.2 3.8 %shard_map.51 = (bf16[192,5120]{1,0:T(8,128)(2,1)}, bf16[72,192]{1,0:T(8,128)(2,1)S(1)}, bf16[72,192]{1,0:T(8,128)(2,1)S(1)}) custom-call(s32[2]{0:T(128)S(1)} %pad_add_fusion.pos_ref, bf16[1440,256]{1,0:T(8,128)(2,1)S(1)} %all_gather.3.wa_ref, bf16[1440,256]{1,0:T(8,128)(2,1)S(1)} %collective-permute-done.wb_ref, bf16[192,5120]{1,0:T(8,128)(2,1)S(1)} %bitcast.8, ...), custom_call_target="tpu_custom_call" | custom-call | tf_op jit(solution)/shard_map/pallas_call | solution.py:131
  45.0 4.9 %all-to-all-start = ((bf16[8,24,5120]{2,1,0:T(8,128)(2,1)}), bf16[8,24,5120]{2,1,0:T(8,128)(2,1)}, u32[]{:S(2)}, u32[]{:S(2)}) async-start(bf16[8,24,5120]{2,1,0:T(8,128)(2,1)} %bitcast.12), calls=%async_computation | async-start | bytes 3932160 | tf_op jit(solution)/shard_map/all_to_all | solution.py:217
  49.9 2.5 %collective-permute-start.2 = (bf16[192,5120]{1,0:T(8,128)(2,1)S(1)}, bf16[192,5120]{1,0:T(8,128)(2,1)S(1)}, u32[]{:S(2)}, u32[]{:S(2)}) collective-permute-start(bf16[192,5120]{1,0:T(8,128)(2,1)S(1)} %bitcast.9), channel_id=1, source_target_pairs={{0,1},{1,0},{2,3},{3,2},{4,5},{5,4},{6,7},{7,6},{8,9},{9,8},{10,11... | collective-permute-start | bytes 5898248 | tf_op jit(solution)/shard_map/ppermute | solution.py:209
  52.5 1.9 %collective-permute-start.1 = (bf16[72,192]{1,0:T(8,128)(2,1)S(1)}, bf16[72,192]{1,0:T(8,128)(2,1)S(1)}, u32[]{:S(2)}, u32[]{:S(2)}) collective-permute-start(bf16[72,192]{1,0:T(8,128)(2,1)S(1)} %get-tuple-element.14), channel_id=1, source_target_pairs={{0,1},{1,0},{2,3},{3,2},{4,5},{5,4},{6,7},{7,6},{8,9},{9,8},{10,11... | collective-permute-start | bytes 82952 | tf_op jit(solution)/shard_map/ppermute | solution.py:209
  54.4 1.7 %collective-permute-done.1.got_ref = bf16[72,192]{1,0:T(8,128)(2,1)S(1)} collective-permute-done((bf16[72,192]{1,0:T(8,128)(2,1)S(1)}, bf16[72,192]{1,0:T(8,128)(2,1)S(1)}, u32[]{:S(2)}, u32[]{:S(2)}) %collective-permute-start.1) | collective-permute-done | bytes 27680 | tf_op jit(solution)/shard_map/ppermute | solution.py:209
  56.1 0.0 collective-permute-done.2.xo_ref
  56.1 1.8 %shard_map.52 = (f32[360,256]{1,0:T(8,128)S(1)}, bf16[360,256]{1,0:T(8,128)(2,1)S(1)}, bf16[360,256]{1,0:T(8,128)(2,1)S(1)}, bf16[360,256]{1,0:T(8,128)(2,1)S(1)}) custom-call(s32[2]{0:T(128)S(1)} %pad_add_fusion.pos_ref, bf16[72,192]{1,0:T(8,128)(2,1)S(1)} %get-tuple-element.13.mine_ref, bf16[72,192]{1,0:T(8,128)(2,1)S(1)} %collective-permute-done.1.got_ref, ...), custom_call_target="tpu_custom_call" | custom-call | tf_op jit(solution)/shard_map/pallas_call | solution.py:173
  57.9 7.3 %collective-permute-start.3 = (bf16[360,256]{1,0:T(8,128)(2,1)S(1)}, bf16[360,256]{1,0:T(8,128)(2,1)S(1)}, u32[]{:S(2)}, u32[]{:S(2)}) collective-permute-start(bf16[360,256]{1,0:T(8,128)(2,1)S(1)} %get-tuple-element.17), channel_id=1, source_target_pairs={{0,4},{2,6},{4,0},{6,2},{1,5},{3,7},{5,1},{7,3},{8,12},{10,14},{12... | collective-permute-start | bytes 552968 | tf_op jit(solution)/shard_map/ppermute | solution.py:205
  65.2 4.8 %collective-permute-start.4 = (bf16[360,256]{1,0:T(8,128)(2,1)S(1)}, bf16[360,256]{1,0:T(8,128)(2,1)S(1)}, u32[]{:S(2)}, u32[]{:S(2)}) collective-permute-start(bf16[360,256]{1,0:T(8,128)(2,1)S(1)} %get-tuple-element.18), channel_id=1, source_target_pairs={{0,2},{2,4},{4,6},{6,0},{1,3},{3,5},{5,7},{7,1},{8,10},{10,12},{12... | collective-permute-start | bytes 552968 | tf_op jit(solution)/shard_map/ppermute | solution.py:205
  69.9 3.5 %collective-permute-start.5 = (bf16[360,256]{1,0:T(8,128)(2,1)S(1)}, bf16[360,256]{1,0:T(8,128)(2,1)S(1)}, u32[]{:S(2)}, u32[]{:S(2)}) collective-permute-start(bf16[360,256]{1,0:T(8,128)(2,1)S(1)} %get-tuple-element.19), channel_id=1, source_target_pairs={{0,6},{2,0},{4,2},{6,4},{1,7},{3,1},{5,3},{7,5},{8,14},{10,8},{12,... | collective-permute-start | bytes 552968 | tf_op jit(solution)/shard_map/ppermute | solution.py:205
  73.5 1.5 %all-to-all-done = bf16[8,24,5120]{2,1,0:T(8,128)(2,1)} async-done(((bf16[8,24,5120]{2,1,0:T(8,128)(2,1)}), bf16[8,24,5120]{2,1,0:T(8,128)(2,1)}, u32[]{:S(2)}, u32[]{:S(2)}) %all-to-all-start) | async-done | bytes 1966112 | tf_op jit(solution)/shard_map/all_to_all | solution.py:217
  75.0 1.9 %reduce_sum.24 = bf16[24,5120]{1,0:T(8,128)(2,1)S(1)} reduce(bf16[8,24,5120]{2,1,0:T(8,128)(2,1)} %all-to-all-done, bf16[]{:T(256)} %constant.11.clone.1), dimensions={0}, to_apply=%region_0.0 | reduce | flops 860160 | bytes 2211842 | tf_op jit(solution)/shard_map/reduce_sum | solution.py:213
  76.9 0.8 reshape.22
  77.7 9.0 %all-to-all-start.1 = ((bf16[12,2,5120]{2,1,0:T(2,128)(2,1)}), bf16[12,2,5120]{2,1,0:T(2,128)(2,1)S(1)}, u32[]{:S(2)}, u32[]{:S(2)}) async-start(bf16[12,2,5120]{2,1,0:T(2,128)(2,1)} %reshape.22), calls=%async_computation.1 | async-start | bytes 491520 | tf_op jit(solution)/shard_map/all_to_all | solution.py:217
  86.7 0.0 collective-permute-done.3.refs_0_
  86.7 0.0 collective-permute-done.4.refs_1_
  86.7 2.4 %collective-permute-done.5.refs_2_ = bf16[360,256]{1,0:T(8,128)(2,1)S(1)} collective-permute-done((bf16[360,256]{1,0:T(8,128)(2,1)S(1)}, bf16[360,256]{1,0:T(8,128)(2,1)S(1)}, u32[]{:S(2)}, u32[]{:S(2)}) %collective-permute-start.5) | collective-permute-done | bytes 184352 | tf_op jit(solution)/shard_map/ppermute | solution.py:205
  89.1 0.8 shard_map.53
  89.9 10.5 %all-to-all-done.1 = bf16[12,2,5120]{2,1,0:T(2,128)(2,1)S(1)} async-done(((bf16[12,2,5120]{2,1,0:T(2,128)(2,1)}), bf16[12,2,5120]{2,1,0:T(2,128)(2,1)S(1)}, u32[]{:S(2)}, u32[]{:S(2)}) %all-to-all-start.1) | async-done | bytes 245792 | tf_op jit(solution)/shard_map/all_to_all | solution.py:217
  100.4 0.8 reduce_sum.25
Async XLA Ops:
  0.6 1.0 copy-start.2
  1.6 39.6 %copy-start = (bf16[1,192,1,5120]{3,1,2,0:T(8,128)(2,1)S(1)}, bf16[1,192,1,5120]{3,1,2,0:T(8,128)(2,1)}, u32[]{:S(2)}) copy-start(bf16[1,192,1,5120]{3,1,2,0:T(8,128)(2,1)} %param.3) | copy-start | bytes 5898244
  1.6 39.6 %copy-start.1 = (bf16[1,192,1,72]{1,3,2,0:T(8,128)(2,1)S(1)}, bf16[1,192,1,72]{1,3,2,0:T(8,128)(2,1)}, u32[]{:S(2)}) copy-start(bf16[1,192,1,72]{1,3,2,0:T(8,128)(2,1)} %param.4) | copy-start | bytes 82948
  36.0 5.1 %collective-permute-start = (bf16[1440,256]{1,0:T(8,128)(2,1)S(1)}, bf16[1440,256]{1,0:T(8,128)(2,1)S(1)}, u32[]{:S(2)}, u32[]{:S(2)}) collective-permute-start(bf16[1440,256]{1,0:T(8,128)(2,1)S(1)} %all_gather.3.wa_ref), channel_id=1, source_target_pairs={{0,1},{1,0},{2,3},{3,2},{4,5},{5,4},{6,7},{7,6},{8,9},{9,8},{10,11... | collective-permute-start | bytes 2211848 | tf_op jit(solution)/shard_map/ppermute | solution.py:209
  45.0 30.0 %all-to-all-start = ((bf16[8,24,5120]{2,1,0:T(8,128)(2,1)}), bf16[8,24,5120]{2,1,0:T(8,128)(2,1)}, u32[]{:S(2)}, u32[]{:S(2)}) async-start(bf16[8,24,5120]{2,1,0:T(8,128)(2,1)} %bitcast.12), calls=%async_computation | async-start | bytes 3932160 | tf_op jit(solution)/shard_map/all_to_all | solution.py:217
  49.9 6.2 %collective-permute-start.2 = (bf16[192,5120]{1,0:T(8,128)(2,1)S(1)}, bf16[192,5120]{1,0:T(8,128)(2,1)S(1)}, u32[]{:S(2)}, u32[]{:S(2)}) collective-permute-start(bf16[192,5120]{1,0:T(8,128)(2,1)S(1)} %bitcast.9), channel_id=1, source_target_pairs={{0,1},{1,0},{2,3},{3,2},{4,5},{5,4},{6,7},{7,6},{8,9},{9,8},{10,11... | collective-permute-start | bytes 5898248 | tf_op jit(solution)/shard_map/ppermute | solution.py:209
  52.5 3.6 %collective-permute-start.1 = (bf16[72,192]{1,0:T(8,128)(2,1)S(1)}, bf16[72,192]{1,0:T(8,128)(2,1)S(1)}, u32[]{:S(2)}, u32[]{:S(2)}) collective-permute-start(bf16[72,192]{1,0:T(8,128)(2,1)S(1)} %get-tuple-element.14), channel_id=1, source_target_pairs={{0,1},{1,0},{2,3},{3,2},{4,5},{5,4},{6,7},{7,6},{8,9},{9,8},{10,11... | collective-permute-start | bytes 82952 | tf_op jit(solution)/shard_map/ppermute | solution.py:209
  57.9 28.8 %collective-permute-start.3 = (bf16[360,256]{1,0:T(8,128)(2,1)S(1)}, bf16[360,256]{1,0:T(8,128)(2,1)S(1)}, u32[]{:S(2)}, u32[]{:S(2)}) collective-permute-start(bf16[360,256]{1,0:T(8,128)(2,1)S(1)} %get-tuple-element.17), channel_id=1, source_target_pairs={{0,4},{2,6},{4,0},{6,2},{1,5},{3,7},{5,1},{7,3},{8,12},{10,14},{12... | collective-permute-start | bytes 552968 | tf_op jit(solution)/shard_map/ppermute | solution.py:205
  65.2 21.5 %collective-permute-start.4 = (bf16[360,256]{1,0:T(8,128)(2,1)S(1)}, bf16[360,256]{1,0:T(8,128)(2,1)S(1)}, u32[]{:S(2)}, u32[]{:S(2)}) collective-permute-start(bf16[360,256]{1,0:T(8,128)(2,1)S(1)} %get-tuple-element.18), channel_id=1, source_target_pairs={{0,2},{2,4},{4,6},{6,0},{1,3},{3,5},{5,7},{7,1},{8,10},{10,12},{12... | collective-permute-start | bytes 552968 | tf_op jit(solution)/shard_map/ppermute | solution.py:205
  69.9 19.1 %collective-permute-start.5 = (bf16[360,256]{1,0:T(8,128)(2,1)S(1)}, bf16[360,256]{1,0:T(8,128)(2,1)S(1)}, u32[]{:S(2)}, u32[]{:S(2)}) collective-permute-start(bf16[360,256]{1,0:T(8,128)(2,1)S(1)} %get-tuple-element.19), channel_id=1, source_target_pairs={{0,6},{2,0},{4,2},{6,4},{1,7},{3,1},{5,3},{7,5},{8,14},{10,8},{12,... | collective-permute-start | bytes 552968 | tf_op jit(solution)/shard_map/ppermute | solution.py:205
  77.7 22.7 %all-to-all-start.1 = ((bf16[12,2,5120]{2,1,0:T(2,128)(2,1)}), bf16[12,2,5120]{2,1,0:T(2,128)(2,1)S(1)}, u32[]{:S(2)}, u32[]{:S(2)}) async-start(bf16[12,2,5120]{2,1,0:T(2,128)(2,1)} %reshape.22), calls=%async_computation.1 | async-start | bytes 491520 | tf_op jit(solution)/shard_map/all_to_all | solution.py:217

commit v5 on v4

--- a/solution.py
+++ b/solution.py
@@ -12,7 +12,7 @@
 LANES = 128
 INTER = ("yh", "yl", "zl", "x")
 FIRST = ("x", "yl")
-SECOND = ("yh", "zl")
+SECOND = ("zl", "yh")
 F32 = jnp.float32
 BF16 = jnp.bfloat16
 VMEM = pl.BlockSpec(memory_space=pltpu.VMEM)

time: 102 us -> 101 us (level)
  waiting for transfers between devices: 17.8 us -> 16.5 us
    all_to_all x2, waiting for transfers between devices: 12 us -> 10.7 us  [spread(): return lax.all_to_all(array, axes, split_axis=0, concat_axis=0, tiled=True)]
where the time goes in v5:
time: 101 us; the launch traced here: 99.9 us
  starting transfers between devices  37.3 us (37%)
  blocking collectives  34.2 us (34%)
  waiting for transfers between devices  16.5 us (16%)
  Pallas kernels  6.55 us (6%)
  other arithmetic  2.76 us (3%)
  local copies, waits for them, and re-layouts  1.77 us (2%)
    all_gather x1, blocking collectives, body(): w_mine = lax.all_gather(own, 'zh', axis=0, tiled=True)  34.2 us
    ppermute x3, starting transfers between devices, step(): return lax.ppermute(array, axis, [(i, (i + by) % n) for i in range(n)])  15.6 us
    all_to_all x2, starting transfers between devices, spread(): return lax.all_to_all(array, axes, split_axis=0, concat_axis=0, tiled=True)  13.9 us
    all_to_all x2, waiting for transfers between devices, spread(): return lax.all_to_all(array, axes, split_axis=0, concat_axis=0, tiled=True)  10.7 us
    ppermute x3, starting transfers between devices, swapped(): return lax.ppermute(array, 'c', [(0, 1), (1, 0)])  7.78 us
    pallas_call x1, Pallas kernels, gate_part(): pl.pallas_call(functools.partial(gate_kernel, orders), out_shape=(pltpu.H...  3.81 us
    ppermute x3, waiting for transfers between devices, swapped(): return lax.ppermute(array, 'c', [(0, 1), (1, 0)])  3.44 us
    reduce_sum x2, other arithmetic, summed_pieces(): return jnp.sum(pieces.astype(F32), axis=0).astype(BF16)  2.68 us
  transfers between devices with their start and end apart: 8, of which 5 were waited for; matrix products, arithmetic and copies ran while one was open for 3% of the time, Pallas kernels for 3%

profile of v5, /device:TPU:1, one launch (start us, length us, event | category | flops | bytes accessed | tf_op | source)
XLA Modules:
  0.0 99.9 jit_solution(15578175317225492188)
XLA Ops:
  0.6 0.0 copy-start.2
  0.6 1.0 copy-done.2
  1.6 0.0 copy-start
  1.6 0.0 copy-start.1
  1.6 0.2 shard_map.50
  1.8 34.2 %all_gather.3.wa_ref = bf16[1440,256]{1,0:T(8,128)(2,1)S(1)} all-gather(bf16[360,256]{1,0:T(8,128)(2,1)S(1)} %shard_map.50), channel_id=1, replica_groups=mesh['yh'=4,'yl'=2,'zl'=3,'x'=4,'zh'=4,'c'=2] {'zh'}, dimensions={0}, use_global_device_ids=true | all-gather | bytes 921600 | tf_op jit(solution)/shard_map/all_gather | solution.py:231
  36.0 3.3 %collective-permute-start = (bf16[1440,256]{1,0:T(8,128)(2,1)S(1)}, bf16[1440,256]{1,0:T(8,128)(2,1)S(1)}, u32[]{:S(2)}, u32[]{:S(2)}) collective-permute-start(bf16[1440,256]{1,0:T(8,128)(2,1)S(1)} %all_gather.3.wa_ref), channel_id=1, source_target_pairs={{0,1},{1,0},{2,3},{3,2},{4,5},{5,4},{6,7},{7,6},{8,9},{9,8},{10,11... | collective-permute-start | bytes 2211848 | tf_op jit(solution)/shard_map/ppermute | solution.py:209
  39.4 0.1 pad_add_fusion.pos_ref
  39.4 1.7 %collective-permute-done.wb_ref = bf16[1440,256]{1,0:T(8,128)(2,1)S(1)} collective-permute-done((bf16[1440,256]{1,0:T(8,128)(2,1)S(1)}, bf16[1440,256]{1,0:T(8,128)(2,1)S(1)}, u32[]{:S(2)}, u32[]{:S(2)}) %collective-permute-start) | collective-permute-done | bytes 737312 | tf_op jit(solution)/shard_map/ppermute | solution.py:209
  41.2 0.0 copy-done
  41.2 0.0 copy-done.1
  41.2 3.8 %shard_map.51 = (bf16[192,5120]{1,0:T(8,128)(2,1)}, bf16[72,192]{1,0:T(8,128)(2,1)S(1)}, bf16[72,192]{1,0:T(8,128)(2,1)S(1)}) custom-call(s32[2]{0:T(128)S(1)} %pad_add_fusion.pos_ref, bf16[1440,256]{1,0:T(8,128)(2,1)S(1)} %all_gather.3.wa_ref, bf16[1440,256]{1,0:T(8,128)(2,1)S(1)} %collective-permute-done.wb_ref, bf16[192,5120]{1,0:T(8,128)(2,1)S(1)} %bitcast.8, ...), custom_call_target="tpu_custom_call" | custom-call | tf_op jit(solution)/shard_map/pallas_call | solution.py:131
  45.0 4.9 %all-to-all-start = ((bf16[8,24,5120]{2,1,0:T(8,128)(2,1)}), bf16[8,24,5120]{2,1,0:T(8,128)(2,1)}, u32[]{:S(2)}, u32[]{:S(2)}) async-start(bf16[8,24,5120]{2,1,0:T(8,128)(2,1)} %bitcast.12), calls=%async_computation | async-start | bytes 3932160 | tf_op jit(solution)/shard_map/all_to_all | solution.py:217
  49.9 2.5 %collective-permute-start.2 = (bf16[192,5120]{1,0:T(8,128)(2,1)S(1)}, bf16[192,5120]{1,0:T(8,128)(2,1)S(1)}, u32[]{:S(2)}, u32[]{:S(2)}) collective-permute-start(bf16[192,5120]{1,0:T(8,128)(2,1)S(1)} %bitcast.9), channel_id=1, source_target_pairs={{0,1},{1,0},{2,3},{3,2},{4,5},{5,4},{6,7},{7,6},{8,9},{9,8},{10,11... | collective-permute-start | bytes 5898248 | tf_op jit(solution)/shard_map/ppermute | solution.py:209
  52.5 1.9 %collective-permute-start.1 = (bf16[72,192]{1,0:T(8,128)(2,1)S(1)}, bf16[72,192]{1,0:T(8,128)(2,1)S(1)}, u32[]{:S(2)}, u32[]{:S(2)}) collective-permute-start(bf16[72,192]{1,0:T(8,128)(2,1)S(1)} %get-tuple-element.14), channel_id=1, source_target_pairs={{0,1},{1,0},{2,3},{3,2},{4,5},{5,4},{6,7},{7,6},{8,9},{9,8},{10,11... | collective-permute-start | bytes 82952 | tf_op jit(solution)/shard_map/ppermute | solution.py:209
  54.4 1.7 %collective-permute-done.1.got_ref = bf16[72,192]{1,0:T(8,128)(2,1)S(1)} collective-permute-done((bf16[72,192]{1,0:T(8,128)(2,1)S(1)}, bf16[72,192]{1,0:T(8,128)(2,1)S(1)}, u32[]{:S(2)}, u32[]{:S(2)}) %collective-permute-start.1) | collective-permute-done | bytes 27680 | tf_op jit(solution)/shard_map/ppermute | solution.py:209
  56.1 0.0 collective-permute-done.2.xo_ref
  56.1 1.8 %shard_map.52 = (f32[360,256]{1,0:T(8,128)S(1)}, bf16[360,256]{1,0:T(8,128)(2,1)S(1)}, bf16[360,256]{1,0:T(8,128)(2,1)S(1)}, bf16[360,256]{1,0:T(8,128)(2,1)S(1)}) custom-call(s32[2]{0:T(128)S(1)} %pad_add_fusion.pos_ref, bf16[72,192]{1,0:T(8,128)(2,1)S(1)} %get-tuple-element.13.mine_ref, bf16[72,192]{1,0:T(8,128)(2,1)S(1)} %collective-permute-done.1.got_ref, ...), custom_call_target="tpu_custom_call" | custom-call | tf_op jit(solution)/shard_map/pallas_call | solution.py:173
  57.8 7.3 %collective-permute-start.3 = (bf16[360,256]{1,0:T(8,128)(2,1)S(1)}, bf16[360,256]{1,0:T(8,128)(2,1)S(1)}, u32[]{:S(2)}, u32[]{:S(2)}) collective-permute-start(bf16[360,256]{1,0:T(8,128)(2,1)S(1)} %get-tuple-element.17), channel_id=1, source_target_pairs={{0,4},{2,6},{4,0},{6,2},{1,5},{3,7},{5,1},{7,3},{8,12},{10,14},{12... | collective-permute-start | bytes 552968 | tf_op jit(solution)/shard_map/ppermute | solution.py:205
  65.2 4.7 %collective-permute-start.4 = (bf16[360,256]{1,0:T(8,128)(2,1)S(1)}, bf16[360,256]{1,0:T(8,128)(2,1)S(1)}, u32[]{:S(2)}, u32[]{:S(2)}) collective-permute-start(bf16[360,256]{1,0:T(8,128)(2,1)S(1)} %get-tuple-element.18), channel_id=1, source_target_pairs={{0,2},{2,4},{4,6},{6,0},{1,3},{3,5},{5,7},{7,1},{8,10},{10,12},{12... | collective-permute-start | bytes 552968 | tf_op jit(solution)/shard_map/ppermute | solution.py:205
  69.9 3.6 %collective-permute-start.5 = (bf16[360,256]{1,0:T(8,128)(2,1)S(1)}, bf16[360,256]{1,0:T(8,128)(2,1)S(1)}, u32[]{:S(2)}, u32[]{:S(2)}) collective-permute-start(bf16[360,256]{1,0:T(8,128)(2,1)S(1)} %get-tuple-element.19), channel_id=1, source_target_pairs={{0,6},{2,0},{4,2},{6,4},{1,7},{3,1},{5,3},{7,5},{8,14},{10,8},{12,... | collective-permute-start | bytes 552968 | tf_op jit(solution)/shard_map/ppermute | solution.py:205
  73.5 1.5 %all-to-all-done = bf16[8,24,5120]{2,1,0:T(8,128)(2,1)} async-done(((bf16[8,24,5120]{2,1,0:T(8,128)(2,1)}), bf16[8,24,5120]{2,1,0:T(8,128)(2,1)}, u32[]{:S(2)}, u32[]{:S(2)}) %all-to-all-start) | async-done | bytes 1966112 | tf_op jit(solution)/shard_map/all_to_all | solution.py:217
  75.0 1.9 %reduce_sum.24 = bf16[24,5120]{1,0:T(8,128)(2,1)S(1)} reduce(bf16[8,24,5120]{2,1,0:T(8,128)(2,1)} %all-to-all-done, bf16[]{:T(256)} %constant.11.clone.1), dimensions={0}, to_apply=%region_0.0 | reduce | flops 860160 | bytes 2211842 | tf_op jit(solution)/shard_map/reduce_sum | solution.py:213
  76.9 0.8 reshape.22
  77.7 9.0 %all-to-all-start.1 = ((bf16[12,2,5120]{2,1,0:T(2,128)(2,1)}), bf16[12,2,5120]{2,1,0:T(2,128)(2,1)S(1)}, u32[]{:S(2)}, u32[]{:S(2)}) async-start(bf16[12,2,5120]{2,1,0:T(2,128)(2,1)} %reshape.22), calls=%async_computation.1 | async-start | bytes 491520 | tf_op jit(solution)/shard_map/all_to_all | solution.py:217
  86.7 0.0 collective-permute-done.3.refs_0_
  86.7 0.0 collective-permute-done.4.refs_1_
  86.7 2.4 %collective-permute-done.5.refs_2_ = bf16[360,256]{1,0:T(8,128)(2,1)S(1)} collective-permute-done((bf16[360,256]{1,0:T(8,128)(2,1)S(1)}, bf16[360,256]{1,0:T(8,128)(2,1)S(1)}, u32[]{:S(2)}, u32[]{:S(2)}) %collective-permute-start.5) | collective-permute-done | bytes 184352 | tf_op jit(solution)/shard_map/ppermute | solution.py:205
  89.1 0.8 shard_map.53
  89.9 9.2 %all-to-all-done.1 = bf16[12,2,5120]{2,1,0:T(2,128)(2,1)S(1)} async-done(((bf16[12,2,5120]{2,1,0:T(2,128)(2,1)}), bf16[12,2,5120]{2,1,0:T(2,128)(2,1)S(1)}, u32[]{:S(2)}, u32[]{:S(2)}) %all-to-all-start.1) | async-done | bytes 245792 | tf_op jit(solution)/shard_map/all_to_all | solution.py:217
  99.1 0.8 reduce_sum.25
Async XLA Ops:
  0.6 1.0 copy-start.2
  1.6 39.6 %copy-start = (bf16[1,192,1,5120]{3,1,2,0:T(8,128)(2,1)S(1)}, bf16[1,192,1,5120]{3,1,2,0:T(8,128)(2,1)}, u32[]{:S(2)}) copy-start(bf16[1,192,1,5120]{3,1,2,0:T(8,128)(2,1)} %param.3) | copy-start | bytes 5898244
  1.6 39.6 %copy-start.1 = (bf16[1,192,1,72]{1,3,2,0:T(8,128)(2,1)S(1)}, bf16[1,192,1,72]{1,3,2,0:T(8,128)(2,1)}, u32[]{:S(2)}) copy-start(bf16[1,192,1,72]{1,3,2,0:T(8,128)(2,1)} %param.4) | copy-start | bytes 82948
  36.0 5.1 %collective-permute-start = (bf16[1440,256]{1,0:T(8,128)(2,1)S(1)}, bf16[1440,256]{1,0:T(8,128)(2,1)S(1)}, u32[]{:S(2)}, u32[]{:S(2)}) collective-permute-start(bf16[1440,256]{1,0:T(8,128)(2,1)S(1)} %all_gather.3.wa_ref), channel_id=1, source_target_pairs={{0,1},{1,0},{2,3},{3,2},{4,5},{5,4},{6,7},{7,6},{8,9},{9,8},{10,11... | collective-permute-start | bytes 2211848 | tf_op jit(solution)/shard_map/ppermute | solution.py:209
  45.0 30.0 %all-to-all-start = ((bf16[8,24,5120]{2,1,0:T(8,128)(2,1)}), bf16[8,24,5120]{2,1,0:T(8,128)(2,1)}, u32[]{:S(2)}, u32[]{:S(2)}) async-start(bf16[8,24,5120]{2,1,0:T(8,128)(2,1)} %bitcast.12), calls=%async_computation | async-start | bytes 3932160 | tf_op jit(solution)/shard_map/all_to_all | solution.py:217
  49.9 6.2 %collective-permute-start.2 = (bf16[192,5120]{1,0:T(8,128)(2,1)S(1)}, bf16[192,5120]{1,0:T(8,128)(2,1)S(1)}, u32[]{:S(2)}, u32[]{:S(2)}) collective-permute-start(bf16[192,5120]{1,0:T(8,128)(2,1)S(1)} %bitcast.9), channel_id=1, source_target_pairs={{0,1},{1,0},{2,3},{3,2},{4,5},{5,4},{6,7},{7,6},{8,9},{9,8},{10,11... | collective-permute-start | bytes 5898248 | tf_op jit(solution)/shard_map/ppermute | solution.py:209
  52.5 3.6 %collective-permute-start.1 = (bf16[72,192]{1,0:T(8,128)(2,1)S(1)}, bf16[72,192]{1,0:T(8,128)(2,1)S(1)}, u32[]{:S(2)}, u32[]{:S(2)}) collective-permute-start(bf16[72,192]{1,0:T(8,128)(2,1)S(1)} %get-tuple-element.14), channel_id=1, source_target_pairs={{0,1},{1,0},{2,3},{3,2},{4,5},{5,4},{6,7},{7,6},{8,9},{9,8},{10,11... | collective-permute-start | bytes 82952 | tf_op jit(solution)/shard_map/ppermute | solution.py:209
  57.8 28.8 %collective-permute-start.3 = (bf16[360,256]{1,0:T(8,128)(2,1)S(1)}, bf16[360,256]{1,0:T(8,128)(2,1)S(1)}, u32[]{:S(2)}, u32[]{:S(2)}) collective-permute-start(bf16[360,256]{1,0:T(8,128)(2,1)S(1)} %get-tuple-element.17), channel_id=1, source_target_pairs={{0,4},{2,6},{4,0},{6,2},{1,5},{3,7},{5,1},{7,3},{8,12},{10,14},{12... | collective-permute-start | bytes 552968 | tf_op jit(solution)/shard_map/ppermute | solution.py:205
  65.2 21.5 %collective-permute-start.4 = (bf16[360,256]{1,0:T(8,128)(2,1)S(1)}, bf16[360,256]{1,0:T(8,128)(2,1)S(1)}, u32[]{:S(2)}, u32[]{:S(2)}) collective-permute-start(bf16[360,256]{1,0:T(8,128)(2,1)S(1)} %get-tuple-element.18), channel_id=1, source_target_pairs={{0,2},{2,4},{4,6},{6,0},{1,3},{3,5},{5,7},{7,1},{8,10},{10,12},{12... | collective-permute-start | bytes 552968 | tf_op jit(solution)/shard_map/ppermute | solution.py:205
  69.9 19.2 %collective-permute-start.5 = (bf16[360,256]{1,0:T(8,128)(2,1)S(1)}, bf16[360,256]{1,0:T(8,128)(2,1)S(1)}, u32[]{:S(2)}, u32[]{:S(2)}) collective-permute-start(bf16[360,256]{1,0:T(8,128)(2,1)S(1)} %get-tuple-element.19), channel_id=1, source_target_pairs={{0,6},{2,0},{4,2},{6,4},{1,7},{3,1},{5,3},{7,5},{8,14},{10,8},{12,... | collective-permute-start | bytes 552968 | tf_op jit(solution)/shard_map/ppermute | solution.py:205
  77.7 21.4 %all-to-all-start.1 = ((bf16[12,2,5120]{2,1,0:T(2,128)(2,1)}), bf16[12,2,5120]{2,1,0:T(2,128)(2,1)S(1)}, u32[]{:S(2)}, u32[]{:S(2)}) async-start(bf16[12,2,5120]{2,1,0:T(2,128)(2,1)} %reshape.22), calls=%async_computation.1 | async-start | bytes 491520 | tf_op jit(solution)/shard_map/all_to_all | solution.py:217

commit v6 on v5

--- a/solution.py
+++ b/solution.py
@@ -209,8 +209,21 @@
     return lax.ppermute(array, "c", [(0, 1), (1, 0)])
 
 
-def summed_pieces(pieces):
-    return jnp.sum(pieces.astype(F32), axis=0).astype(BF16)
+def sum_kernel(pieces_ref, out_ref):
+    total = pieces_ref[0].astype(F32)
+    for i in range(1, pieces_ref.shape[0]):
+        total = total + pieces_ref[i].astype(F32)
+    out_ref[...] = total.astype(BF16).reshape(out_ref.shape)
+
+
+def summed_pieces(pieces, shape):
+    return pl.pallas_call(
+        sum_kernel,
+        out_shape=pltpu.HBM(shape, BF16),
+        in_specs=[VMEM],
+        out_specs=VMEM,
+        compiler_params=PARAMS,
+    )(pieces)
 
 
 def spread(array, axes):
@@ -243,9 +256,11 @@
     total, *chunks = weight_grad_part(steps, pos, keep, got, x, x_other, chunk, block)
     rows, _ = lax.optimization_barrier((rows, chunks))
     arrived = [step(piece, "zh", dz) for piece, dz in zip(chunks, steps[1:])]
-    rows = summed_pieces(rows)
-    rows = spread(rows.reshape(second, -1, width), SECOND)
-    input_grad = summed_pieces(rows).reshape(1, -1, activations.shape[2], width)
+    left = tok // (first * second)
+    rows = summed_pieces(rows, (second, left, width))
+    rows = spread(rows, SECOND)
+    rows = jnp.sum(rows.astype(F32), axis=0).astype(BF16)
+    input_grad = rows.reshape(1, left, activations.shape[2], width)
     scale = 1.0 / math.sqrt(tok * n_z * lax.axis_size("c"))
     weight_grad = scaled_total(scale, total, arrived)
     return (weight_grad, input_grad)

time: 101 us -> 101 us (level)
  Pallas kernels: 6.55 us -> 9.1 us
  other arithmetic: 2.76 us -> 0.89 us
    pallas_call x0 -> x1, Pallas kernels: none -> 2.53 us  [summed_pieces(): pl.pallas_call(sum_kernel, out_shape=pltpu.HBM(shape, BF16), in_specs=[VM...]
    reduce_sum x2 -> x1, other arithmetic: 2.68 us -> 0.82 us  [body(): rows = jnp.sum(rows.astype(F32), axis=0).astype(BF16)]
  transfers between devices with their start and end apart: 8 -> 8, of which waited for: 5 -> 5; matrix products, arithmetic and copies ran while one was open for 3% -> 0% of each run, Pallas kernels for 3% -> 5%
where the time goes in v6:
time: 101 us; the launch traced here: 99.9 us
  starting transfers between devices  37.3 us (37%)
  blocking collectives  34.2 us (34%)
  waiting for transfers between devices  16.6 us (16%)
  Pallas kernels  9.1 us (9%)
    all_gather x1, blocking collectives, body(): w_mine = lax.all_gather(own, 'zh', axis=0, tiled=True)  34.2 us
    ppermute x3, starting transfers between devices, step(): return lax.ppermute(array, axis, [(i, (i + by) % n) for i in range(n)])  15.6 us
    all_to_all x2, starting transfers between devices, spread(): return lax.all_to_all(array, axes, split_axis=0, concat_axis=0, tiled=True)  13.9 us
    all_to_all x2, waiting for transfers between devices, spread(): return lax.all_to_all(array, axes, split_axis=0, concat_axis=0, tiled=True)  10.6 us
    ppermute x3, starting transfers between devices, swapped(): return lax.ppermute(array, 'c', [(0, 1), (1, 0)])  7.78 us
    pallas_call x1, Pallas kernels, gate_part(): pl.pallas_call(functools.partial(gate_kernel, orders), out_shape=(pltpu.H...  3.81 us
    ppermute x3, waiting for transfers between devices, swapped(): return lax.ppermute(array, 'c', [(0, 1), (1, 0)])  3.44 us
    pallas_call x1, Pallas kernels, summed_pieces(): pl.pallas_call(sum_kernel, out_shape=pltpu.HBM(shape, BF16), in_specs=[VM...  2.53 us
  transfers between devices with their start and end apart: 8, of which 5 were waited for; matrix products, arithmetic and copies ran while one was open for 0% of the time, Pallas kernels for 5%

profile of v6, /device:TPU:1, one launch (start us, length us, event | category | flops | bytes accessed | tf_op | source)
XLA Modules:
  0.0 99.9 jit_solution(12868564884285482587)
XLA Ops:
  0.6 0.0 copy-start.2
  0.6 1.0 copy-done.2
  1.6 0.0 copy-start
  1.6 0.0 copy-start.1
  1.6 0.2 shard_map.50
  1.8 34.2 %all_gather.3.wa_ref = bf16[1440,256]{1,0:T(8,128)(2,1)S(1)} all-gather(bf16[360,256]{1,0:T(8,128)(2,1)S(1)} %shard_map.50), channel_id=1, replica_groups=mesh['yh'=4,'yl'=2,'zl'=3,'x'=4,'zh'=4,'c'=2] {'zh'}, dimensions={0}, use_global_device_ids=true | all-gather | bytes 921600 | tf_op jit(solution)/shard_map/all_gather | solution.py:244
  36.0 3.3 %collective-permute-start = (bf16[1440,256]{1,0:T(8,128)(2,1)S(1)}, bf16[1440,256]{1,0:T(8,128)(2,1)S(1)}, u32[]{:S(2)}, u32[]{:S(2)}) collective-permute-start(bf16[1440,256]{1,0:T(8,128)(2,1)S(1)} %all_gather.3.wa_ref), channel_id=1, source_target_pairs={{0,1},{1,0},{2,3},{3,2},{4,5},{5,4},{6,7},{7,6},{8,9},{9,8},{10,11... | collective-permute-start | bytes 2211848 | tf_op jit(solution)/shard_map/ppermute | solution.py:209
  39.4 0.1 pad_add_fusion.pos_ref
  39.4 1.7 %collective-permute-done.wb_ref = bf16[1440,256]{1,0:T(8,128)(2,1)S(1)} collective-permute-done((bf16[1440,256]{1,0:T(8,128)(2,1)S(1)}, bf16[1440,256]{1,0:T(8,128)(2,1)S(1)}, u32[]{:S(2)}, u32[]{:S(2)}) %collective-permute-start) | collective-permute-done | bytes 737312 | tf_op jit(solution)/shard_map/ppermute | solution.py:209
  41.2 0.0 copy-done
  41.2 0.0 copy-done.1
  41.2 3.8 %shard_map.51 = (bf16[192,5120]{1,0:T(8,128)(2,1)}, bf16[72,192]{1,0:T(8,128)(2,1)S(1)}, bf16[72,192]{1,0:T(8,128)(2,1)S(1)}) custom-call(s32[2]{0:T(128)S(1)} %pad_add_fusion.pos_ref, bf16[1440,256]{1,0:T(8,128)(2,1)S(1)} %all_gather.3.wa_ref, bf16[1440,256]{1,0:T(8,128)(2,1)S(1)} %collective-permute-done.wb_ref, bf16[192,5120]{1,0:T(8,128)(2,1)S(1)} %bitcast.8, ...), custom_call_target="tpu_custom_call" | custom-call | tf_op jit(solution)/shard_map/pallas_call | solution.py:131
  45.0 4.9 %all-to-all-start = ((bf16[8,24,5120]{2,1,0:T(8,128)(2,1)}), bf16[8,24,5120]{2,1,0:T(8,128)(2,1)}, u32[]{:S(2)}, u32[]{:S(2)}) async-start(bf16[8,24,5120]{2,1,0:T(8,128)(2,1)} %bitcast.12), calls=%async_computation | async-start | bytes 3932160 | tf_op jit(solution)/shard_map/all_to_all | solution.py:230
  49.9 2.5 %collective-permute-start.2 = (bf16[192,5120]{1,0:T(8,128)(2,1)S(1)}, bf16[192,5120]{1,0:T(8,128)(2,1)S(1)}, u32[]{:S(2)}, u32[]{:S(2)}) collective-permute-start(bf16[192,5120]{1,0:T(8,128)(2,1)S(1)} %bitcast.9), channel_id=1, source_target_pairs={{0,1},{1,0},{2,3},{3,2},{4,5},{5,4},{6,7},{7,6},{8,9},{9,8},{10,11... | collective-permute-start | bytes 5898248 | tf_op jit(solution)/shard_map/ppermute | solution.py:209
  52.5 1.9 %collective-permute-start.1 = (bf16[72,192]{1,0:T(8,128)(2,1)S(1)}, bf16[72,192]{1,0:T(8,128)(2,1)S(1)}, u32[]{:S(2)}, u32[]{:S(2)}) collective-permute-start(bf16[72,192]{1,0:T(8,128)(2,1)S(1)} %get-tuple-element.14), channel_id=1, source_target_pairs={{0,1},{1,0},{2,3},{3,2},{4,5},{5,4},{6,7},{7,6},{8,9},{9,8},{10,11... | collective-permute-start | bytes 82952 | tf_op jit(solution)/shard_map/ppermute | solution.py:209
  54.4 1.7 %collective-permute-done.1.got_ref = bf16[72,192]{1,0:T(8,128)(2,1)S(1)} collective-permute-done((bf16[72,192]{1,0:T(8,128)(2,1)S(1)}, bf16[72,192]{1,0:T(8,128)(2,1)S(1)}, u32[]{:S(2)}, u32[]{:S(2)}) %collective-permute-start.1) | collective-permute-done | bytes 27680 | tf_op jit(solution)/shard_map/ppermute | solution.py:209
  56.1 0.0 collective-permute-done.2.xo_ref
  56.1 1.8 %shard_map.52 = (f32[360,256]{1,0:T(8,128)S(1)}, bf16[360,256]{1,0:T(8,128)(2,1)S(1)}, bf16[360,256]{1,0:T(8,128)(2,1)S(1)}, bf16[360,256]{1,0:T(8,128)(2,1)S(1)}) custom-call(s32[2]{0:T(128)S(1)} %pad_add_fusion.pos_ref, bf16[72,192]{1,0:T(8,128)(2,1)S(1)} %get-tuple-element.13.mine_ref, bf16[72,192]{1,0:T(8,128)(2,1)S(1)} %collective-permute-done.1.got_ref, ...), custom_call_target="tpu_custom_call" | custom-call | tf_op jit(solution)/shard_map/pallas_call | solution.py:173
  57.9 7.4 %collective-permute-start.3 = (bf16[360,256]{1,0:T(8,128)(2,1)S(1)}, bf16[360,256]{1,0:T(8,128)(2,1)S(1)}, u32[]{:S(2)}, u32[]{:S(2)}) collective-permute-start(bf16[360,256]{1,0:T(8,128)(2,1)S(1)} %get-tuple-element.17), channel_id=1, source_target_pairs={{0,4},{2,6},{4,0},{6,2},{1,5},{3,7},{5,1},{7,3},{8,12},{10,14},{12... | collective-permute-start | bytes 552968 | tf_op jit(solution)/shard_map/ppermute | solution.py:205
  65.2 4.7 %collective-permute-start.4 = (bf16[360,256]{1,0:T(8,128)(2,1)S(1)}, bf16[360,256]{1,0:T(8,128)(2,1)S(1)}, u32[]{:S(2)}, u32[]{:S(2)}) collective-permute-start(bf16[360,256]{1,0:T(8,128)(2,1)S(1)} %get-tuple-element.18), channel_id=1, source_target_pairs={{0,2},{2,4},{4,6},{6,0},{1,3},{3,5},{5,7},{7,1},{8,10},{10,12},{12... | collective-permute-start | bytes 552968 | tf_op jit(solution)/shard_map/ppermute | solution.py:205
  69.9 3.6 %collective-permute-start.5 = (bf16[360,256]{1,0:T(8,128)(2,1)S(1)}, bf16[360,256]{1,0:T(8,128)(2,1)S(1)}, u32[]{:S(2)}, u32[]{:S(2)}) collective-permute-start(bf16[360,256]{1,0:T(8,128)(2,1)S(1)} %get-tuple-element.19), channel_id=1, source_target_pairs={{0,6},{2,0},{4,2},{6,4},{1,7},{3,1},{5,3},{7,5},{8,14},{10,8},{12,... | collective-permute-start | bytes 552968 | tf_op jit(solution)/shard_map/ppermute | solution.py:205
  73.5 1.5 %all-to-all-done.pieces_ref = bf16[8,24,5120]{2,1,0:T(8,128)(2,1)} async-done(((bf16[8,24,5120]{2,1,0:T(8,128)(2,1)}), bf16[8,24,5120]{2,1,0:T(8,128)(2,1)}, u32[]{:S(2)}, u32[]{:S(2)}) %all-to-all-start) | async-done | bytes 1966112 | tf_op jit(solution)/shard_map/all_to_all | solution.py:230
  75.0 2.5 %shard_map.54 = bf16[12,2,5120]{2,1,0:T(2,128)(2,1)} custom-call(bf16[8,24,5120]{2,1,0:T(8,128)(2,1)} %all-to-all-done.pieces_ref), custom_call_target="tpu_custom_call" | custom-call | tf_op jit(solution)/shard_map/pallas_call | solution.py:220
  77.5 9.0 %all-to-all-start.1 = ((bf16[12,2,5120]{2,1,0:T(2,128)(2,1)}), bf16[12,2,5120]{2,1,0:T(2,128)(2,1)S(1)}, u32[]{:S(2)}, u32[]{:S(2)}) async-start(bf16[12,2,5120]{2,1,0:T(2,128)(2,1)} %shard_map.54), calls=%async_computation.1 | async-start | bytes 491520 | tf_op jit(solution)/shard_map/all_to_all | solution.py:230
  86.6 0.0 collective-permute-done.3.refs_0_
  86.6 0.0 collective-permute-done.4.refs_1_
  86.6 2.5 %collective-permute-done.5.refs_2_ = bf16[360,256]{1,0:T(8,128)(2,1)S(1)} collective-permute-done((bf16[360,256]{1,0:T(8,128)(2,1)S(1)}, bf16[360,256]{1,0:T(8,128)(2,1)S(1)}, u32[]{:S(2)}, u32[]{:S(2)}) %collective-permute-start.5) | collective-permute-done | bytes 184352 | tf_op jit(solution)/shard_map/ppermute | solution.py:205
  89.1 0.8 shard_map.53
  90.0 9.1 %all-to-all-done.1 = bf16[12,2,5120]{2,1,0:T(2,128)(2,1)S(1)} async-done(((bf16[12,2,5120]{2,1,0:T(2,128)(2,1)}), bf16[12,2,5120]{2,1,0:T(2,128)(2,1)S(1)}, u32[]{:S(2)}, u32[]{:S(2)}) %all-to-all-start.1) | async-done | bytes 245792 | tf_op jit(solution)/shard_map/all_to_all | solution.py:230
  99.1 0.8 reduce_sum.12
Async XLA Ops:
  0.6 1.0 copy-start.2
  1.6 39.6 %copy-start = (bf16[1,192,1,5120]{3,1,2,0:T(8,128)(2,1)S(1)}, bf16[1,192,1,5120]{3,1,2,0:T(8,128)(2,1)}, u32[]{:S(2)}) copy-start(bf16[1,192,1,5120]{3,1,2,0:T(8,128)(2,1)} %param.3) | copy-start | bytes 5898244
  1.6 39.6 %copy-start.1 = (bf16[1,192,1,72]{1,3,2,0:T(8,128)(2,1)S(1)}, bf16[1,192,1,72]{1,3,2,0:T(8,128)(2,1)}, u32[]{:S(2)}) copy-start(bf16[1,192,1,72]{1,3,2,0:T(8,128)(2,1)} %param.4) | copy-start | bytes 82948
  36.0 5.1 %collective-permute-start = (bf16[1440,256]{1,0:T(8,128)(2,1)S(1)}, bf16[1440,256]{1,0:T(8,128)(2,1)S(1)}, u32[]{:S(2)}, u32[]{:S(2)}) collective-permute-start(bf16[1440,256]{1,0:T(8,128)(2,1)S(1)} %all_gather.3.wa_ref), channel_id=1, source_target_pairs={{0,1},{1,0},{2,3},{3,2},{4,5},{5,4},{6,7},{7,6},{8,9},{9,8},{10,11... | collective-permute-start | bytes 2211848 | tf_op jit(solution)/shard_map/ppermute | solution.py:209
  45.0 30.0 %all-to-all-start = ((bf16[8,24,5120]{2,1,0:T(8,128)(2,1)}), bf16[8,24,5120]{2,1,0:T(8,128)(2,1)}, u32[]{:S(2)}, u32[]{:S(2)}) async-start(bf16[8,24,5120]{2,1,0:T(8,128)(2,1)} %bitcast.12), calls=%async_computation | async-start | bytes 3932160 | tf_op jit(solution)/shard_map/all_to_all | solution.py:230
  49.9 6.2 %collective-permute-start.2 = (bf16[192,5120]{1,0:T(8,128)(2,1)S(1)}, bf16[192,5120]{1,0:T(8,128)(2,1)S(1)}, u32[]{:S(2)}, u32[]{:S(2)}) collective-permute-start(bf16[192,5120]{1,0:T(8,128)(2,1)S(1)} %bitcast.9), channel_id=1, source_target_pairs={{0,1},{1,0},{2,3},{3,2},{4,5},{5,4},{6,7},{7,6},{8,9},{9,8},{10,11... | collective-permute-start | bytes 5898248 | tf_op jit(solution)/shard_map/ppermute | solution.py:209
  52.5 3.6 %collective-permute-start.1 = (bf16[72,192]{1,0:T(8,128)(2,1)S(1)}, bf16[72,192]{1,0:T(8,128)(2,1)S(1)}, u32[]{:S(2)}, u32[]{:S(2)}) collective-permute-start(bf16[72,192]{1,0:T(8,128)(2,1)S(1)} %get-tuple-element.14), channel_id=1, source_target_pairs={{0,1},{1,0},{2,3},{3,2},{4,5},{5,4},{6,7},{7,6},{8,9},{9,8},{10,11... | collective-permute-start | bytes 82952 | tf_op jit(solution)/shard_map/ppermute | solution.py:209
  57.9 28.7 %collective-permute-start.3 = (bf16[360,256]{1,0:T(8,128)(2,1)S(1)}, bf16[360,256]{1,0:T(8,128)(2,1)S(1)}, u32[]{:S(2)}, u32[]{:S(2)}) collective-permute-start(bf16[360,256]{1,0:T(8,128)(2,1)S(1)} %get-tuple-element.17), channel_id=1, source_target_pairs={{0,4},{2,6},{4,0},{6,2},{1,5},{3,7},{5,1},{7,3},{8,12},{10,14},{12... | collective-permute-start | bytes 552968 | tf_op jit(solution)/shard_map/ppermute | solution.py:205
  65.2 21.4 %collective-permute-start.4 = (bf16[360,256]{1,0:T(8,128)(2,1)S(1)}, bf16[360,256]{1,0:T(8,128)(2,1)S(1)}, u32[]{:S(2)}, u32[]{:S(2)}) collective-permute-start(bf16[360,256]{1,0:T(8,128)(2,1)S(1)} %get-tuple-element.18), channel_id=1, source_target_pairs={{0,2},{2,4},{4,6},{6,0},{1,3},{3,5},{5,7},{7,1},{8,10},{10,12},{12... | collective-permute-start | bytes 552968 | tf_op jit(solution)/shard_map/ppermute | solution.py:205
  69.9 19.2 %collective-permute-start.5 = (bf16[360,256]{1,0:T(8,128)(2,1)S(1)}, bf16[360,256]{1,0:T(8,128)(2,1)S(1)}, u32[]{:S(2)}, u32[]{:S(2)}) collective-permute-start(bf16[360,256]{1,0:T(8,128)(2,1)S(1)} %get-tuple-element.19), channel_id=1, source_target_pairs={{0,6},{2,0},{4,2},{6,4},{1,7},{3,1},{5,3},{7,5},{8,14},{10,8},{12,... | collective-permute-start | bytes 552968 | tf_op jit(solution)/shard_map/ppermute | solution.py:205
  77.5 21.6 %all-to-all-start.1 = ((bf16[12,2,5120]{2,1,0:T(2,128)(2,1)}), bf16[12,2,5120]{2,1,0:T(2,128)(2,1)S(1)}, u32[]{:S(2)}, u32[]{:S(2)}) async-start(bf16[12,2,5120]{2,1,0:T(2,128)(2,1)} %shard_map.54), calls=%async_computation.1 | async-start | bytes 491520 | tf_op jit(solution)/shard_map/all_to_all | solution.py:230
